TPU v7x, 256 devices: a whole 4x4x8 slice. The times are simulated.
256 devices in a mesh: dom: 128 (over y, z, x), sub: 2 (over core).
Axes of the slice: x: 4, y: 4, z: 8, core: 2. Of those that a mesh axis runs over, the one named last changes fastest.
Arguments:
- rhs: float32 [64, 8, 32768], P(None, None, ('dom', 'sub')), may hold values from -4.5 to 4.5
- inner_tiles: bfloat16 [4, 64, 64, 32768], P(None, None, None, ('dom', 'sub')), may hold values from -0.2 to 1.2, as said below
- inner_cols: int32 [4, 32768], P(None, ('dom', 'sub')), may hold values from 0 to 127, as said below
- send_blocks: int32 [16384], P(('dom', 'sub')), may hold values from 0 to 127
- face_rows: int32 [16384], P(('dom', 'sub')), may hold values from 0 to 127
- face_counts: int32 [256, 2], P(('dom', 'sub')), may hold values from 0 to 32, as said below
- face_tiles: bfloat16 [64, 64, 16384], P(None, None, ('dom', 'sub')), may hold values from -0.1796875 to 0.1796875
- contact_send: int32 [16384], P(('dom', 'sub')), may hold values from 0 to 127
- contact_rows: int32 [16384], P(('dom', 'sub')), may hold values from 0 to 127
- contact_pair: int32 [256, 64], P(('dom', 'sub')), may hold values from 0 to 63, each once within a row
- contact_tiles: bfloat16 [64, 64, 16384], P(None, None, ('dom', 'sub')), may hold values from -0.1796875 to 0.1796875
Outputs:
- adjoint: float32 [64, 8, 32768], P(None, None, ('dom', 'sub'))
- residual: float32 [64, 8, 32768], P(None, None, ('dom', 'sub'))
- normal_residual: float32 [64, 8, 32768], P(None, None, ('dom', 'sub'))
Inputs may be any that keep to these rules, and one draw needn't show every extreme that they name: `inner_tiles`: the diagonal tile of each row is the identity plus small entries. `inner_cols`: row 0 names the row's own block. `face_counts`: 0 toward a piece that does not exist; 32 is reached on some piece.
All inputs are finite; a program needn't handle non-finite values.
Results may differ from a plain program's by a relative error of at most 0.003.
Values may be sent and summed in bfloat16 or wider, within the bound.
A program may use at most 128 MiB of HBM per device.

v0:
```python
import jax
import jax.numpy as jnp
from jax import lax
from jax.sharding import PartitionSpec as P

ITERS = 2


def with_halo(value, sides, width):
    for axis, dim in sides:
        peers, length = (lax.axis_size(axis), value.shape[dim])
        up = [(i, (i + 1) % peers) for i in range(peers - 1)]
        down = [(j, i) for i, j in up]
        last = lax.slice_in_dim(value, length - width, length, axis=dim)
        initial = lax.slice_in_dim(value, 0, width, axis=dim)
        before = lax.ppermute(last, axis, up)
        after = lax.ppermute(initial, axis, down)
        value = jnp.concatenate([before, value, after], axis=dim)
    return value


def from_partner(value, axis, bit):
    return lax.ppermute(value, axis, [(i, i ^ 1 << bit) for i in range(lax.axis_size(axis))])


def tile_apply(form, tiles, vectors):
    return jnp.einsum(form, tiles.astype(jnp.float32), vectors, precision=lax.Precision.HIGHEST)


def local_inner(left, right):
    return jnp.sum(left * right, axis=(0, 2))


def shards(
    rhs,
    inner_tiles,
    inner_cols,
    send_blocks,
    face_rows,
    face_counts,
    face_tiles,
    contact_send,
    contact_rows,
    contact_pair,
    contact_tiles,
):
    slots = send_blocks.shape[0]
    half = slots // 2
    contacts = contact_send.shape[0]
    depth = inner_tiles.shape[0]
    order = jnp.arange(slots, dtype=jnp.int32)
    side = order // half
    limit = jnp.where(side == 0, face_counts[0, 0], face_counts[0, 1])
    face_mask = (order - side * half < limit).astype(jnp.float32)
    partner_bit = lax.axis_size(("dom", "sub")).bit_length() - 2
    pairing = contact_pair[0]
    slot_range = jnp.arange(contacts, dtype=jnp.int32)
    pair_match = pairing[:, None] == slot_range[None, :]
    pair_onehot = pair_match.astype(jnp.float32)

    def swap_faces(buffer):
        widened = with_halo(buffer, ((("dom", "sub"), 2),), half)
        return jnp.concatenate([widened[:, :, :half], widened[:, :, 3 * half :]], axis=2)

    def swap_contact(buffer):
        return from_partner(buffer, ("dom", "sub"), partner_bit)

    def total_squares(field):
        return lax.psum(local_inner(field, field), ("dom", "sub"))

    def transpose(field):
        result = jnp.zeros_like(field)
        face_source = jnp.take(field, face_rows, axis=2)
        for index in range(depth):
            result = result.at[:, :, inner_cols[index]].add(
                tile_apply("abj,anj->bnj", inner_tiles[index], field)
            )
        products = tile_apply("abq,anq->bnq", face_tiles, face_source) * face_mask[None, None, :]
        returned = swap_faces(products)
        contact_terms = tile_apply(
            "abm,anm->bnm", contact_tiles, jnp.take(field, contact_rows, axis=2)
        )
        outgoing = jnp.einsum(
            "bnm,mk->bnk", contact_terms, pair_onehot, precision=lax.Precision.HIGHEST
        )
        contact_back = swap_contact(outgoing)
        result = result.at[:, :, send_blocks].add(returned)
        result = result.at[:, :, contact_send].add(contact_back)
        return result

    adjoint = jnp.zeros_like(rhs)
    residual = rhs
    normal_residual = transpose(residual)
    direction = normal_residual
    norm_now = total_squares(normal_residual)
    for step in range(ITERS):
        forward_result = jnp.zeros_like(direction)
        for forward_index in range(depth):
            gathered = jnp.take(direction, inner_cols[forward_index], axis=2)
            forward_result = forward_result + tile_apply(
                "abj,bnj->anj", inner_tiles[forward_index], gathered
            )
        received = swap_faces(jnp.take(direction, send_blocks, axis=2))
        face_terms = tile_apply("abq,bnq->anq", face_tiles, received) * face_mask[None, None, :]
        forward_result = forward_result.at[:, :, face_rows].add(face_terms)
        partner_rows = swap_contact(jnp.take(direction, contact_send, axis=2))
        matched = jnp.take(partner_rows, pairing, axis=2)
        forward_result = forward_result.at[:, :, contact_rows].add(
            tile_apply("abm,bnm->anm", contact_tiles, matched)
        )
        curvature = lax.psum(local_inner(forward_result, forward_result), ("dom", "sub"))
        alpha = (norm_now / curvature)[None, :, None]
        adjoint = adjoint + alpha * direction
        residual = residual - alpha * forward_result
        normal_residual = transpose(residual)
        if step + 1 < ITERS:
            norm_next = total_squares(normal_residual)
            direction = normal_residual + (norm_next / norm_now)[None, :, None] * direction
            norm_now = norm_next
    return (adjoint, residual, normal_residual)


def solution(mesh):
    return jax.shard_map(
        shards,
        mesh=mesh,
        in_specs=(
            P(None, None, ("dom", "sub")),
            P(None, None, None, ("dom", "sub")),
            P(None, ("dom", "sub")),
            P(("dom", "sub")),
            P(("dom", "sub")),
            P(("dom", "sub"), None),
            P(None, None, ("dom", "sub")),
            P(("dom", "sub")),
            P(("dom", "sub")),
            P(("dom", "sub"), None),
            P(None, None, ("dom", "sub")),
        ),
        out_specs=(
            P(None, None, ("dom", "sub")),
            P(None, None, ("dom", "sub")),
            P(None, None, ("dom", "sub")),
        ),
        check_vma=False,
    )
```

profile of v0, /device:TPU:1, one launch (start us, length us, event | category | flops | bytes accessed | tf_op | source)
XLA Modules:
  0.0 616.7 jit_solution(3551660699248692701)
XLA Ops:
  8.6 5.1 collective-permute-start.1
  51.0 4.8 copy.66
  65.7 9.6 %scatter_fusion = f32[64,8,128]{0,1,2:T(8,128)S(1)} fusion(f32[64,8,128]{0,1,2:T(8,128)S(1)} %broadcast.133.clone, s32[128]{0:T(128)} %get-tuple-element.44, f32[128,64,8]{1,2,0:T(8,128)} %fusion.38), kind=kCustom, calls=%fused_computation.20 | custom fusion | flops 65536 | bytes 786944 | tf_op jit(solution)/shard_map/scatter-add | solution.py:75
  75.3 9.8 %scatter_fusion.1 = f32[64,8,128]{0,1,2:T(8,128)S(1)} fusion(f32[64,8,128]{0,1,2:T(8,128)S(1)} %scatter_fusion, s32[128]{0:T(128)} %get-tuple-element.43, f32[128,64,8]{1,2,0:T(8,128)} %fusion.28), kind=kCustom, calls=%fused_computation.21 | custom fusion | flops 65536 | bytes 786944 | tf_op jit(solution)/shard_map/scatter-add | solution.py:75
  85.1 9.5 %scatter_fusion.2 = f32[64,8,128]{0,1,2:T(8,128)S(1)} fusion(f32[64,8,128]{0,1,2:T(8,128)S(1)} %scatter_fusion.1, s32[128]{0:T(128)S(1)} %get-tuple-element.45, f32[128,64,8]{1,2,0:T(8,128)} %fusion.18), kind=kCustom, calls=%fused_computation.22 | custom fusion | flops 65536 | bytes 786944 | tf_op jit(solution)/shard_map/scatter-add | solution.py:75
  94.6 9.5 %scatter_fusion.3 = f32[64,8,128]{0,1,2:T(8,128)S(1)} fusion(f32[64,8,128]{0,1,2:T(8,128)S(1)} %scatter_fusion.2, s32[128]{0:T(128)S(1)} %get-tuple-element.42, f32[128,64,8]{1,2,0:T(8,128)} %fusion.8), kind=kCustom, calls=%fused_computation.23 | custom fusion | flops 65536 | bytes 786944 | tf_op jit(solution)/shard_map/scatter-add | solution.py:75
  121.0 8.5 %collective-permute-start.4 = (f32[64,8,32]{0,1,2:T(8,128)}, f32[64,8,32]{0,1,2:T(8,128)S(1)}, u32[]{:S(2)}, u32[]{:S(2)}) collective-permute-start(f32[64,8,32]{0,1,2:T(8,128)} %get-tuple-element.33), channel_id=1, source_target_pairs={{1,0},{2,1},{3,2},{4,3},{5,4},{6,5},{7,6},{8,7},{9,8},{10,9},{11,1... | collective-permute-start | bytes 196616 | tf_op jit(solution)/shard_map/ppermute | solution.py:17
  133.8 5.2 fusion.6
  153.6 7.5 %scatter_fusion.6 = f32[64,8,128]{0,1,2:T(8,128)} fusion(f32[64,8,128]{0,1,2:T(8,128)} %fusion.73, s32[64]{0:T(128)} %copy-done.50, f32[64,64,8]{1,2,0:T(8,128)S(1)} %fusion.91), kind=kCustom, calls=%fused_computation.26 | custom fusion | flops 32768 | bytes 393472 | tf_op jit(solution)/shard_map/scatter-add | solution.py:105
  166.5 7.5 %scatter_fusion.7 = f32[64,8,128]{0,1,2:T(8,128)} fusion(f32[64,8,128]{0,1,2:T(8,128)} %scatter_fusion.6, s32[64]{0:T(128)} %copy-done.52, f32[64,64,8]{1,2,0:T(8,128)} %convolution_bitcast_fusion.1), kind=kCustom, calls=%fused_computation.27 | custom fusion | flops 32768 | bytes 393472 | tf_op jit(solution)/shard_map/scatter-add | solution.py:108
  175.3 82.2 %all-reduce = (f32[8]{0:T(128)S(1)}, f32[8]{0:T(128)S(1)}) all-reduce(f32[8]{0:T(128)S(1)} %copy-done.65, f32[8]{0:T(128)S(1)} %multiply_reduce_fusion.2), channel_id=1, replica_groups=mesh['dom'=128,'sub'=2] {'dom','sub'}, use_global_device_ids=true, to_apply=%region_7.9 | all-reduce | flops 16 | bytes 128 | tf_op jit(solution)/shard_map/psum | solution.py:69
  290.4 9.5 %scatter_fusion.8 = f32[64,8,128]{0,1,2:T(8,128)S(1)} fusion(f32[64,8,128]{0,1,2:T(8,128)S(1)} %broadcast.133.clone.1, s32[128]{0:T(128)S(1)} %copy-done.35, f32[128,64,8]{1,2,0:T(8,128)} %fusion.40), kind=kCustom, calls=%fused_computation.28 | custom fusion | flops 65536 | bytes 786944 | tf_op jit(solution)/shard_map/scatter-add | solution.py:75
  299.9 9.5 %scatter_fusion.9 = f32[64,8,128]{0,1,2:T(8,128)S(1)} fusion(f32[64,8,128]{0,1,2:T(8,128)S(1)} %scatter_fusion.8, s32[128]{0:T(128)S(1)} %copy-done.33, f32[128,64,8]{1,2,0:T(8,128)} %fusion.46), kind=kCustom, calls=%fused_computation.29 | custom fusion | flops 65536 | bytes 786944 | tf_op jit(solution)/shard_map/scatter-add | solution.py:75
  309.4 9.5 %scatter_fusion.10 = f32[64,8,128]{0,1,2:T(8,128)S(1)} fusion(f32[64,8,128]{0,1,2:T(8,128)S(1)} %scatter_fusion.9, s32[128]{0:T(128)S(1)} %get-tuple-element.45, f32[128,64,8]{1,2,0:T(8,128)} %fusion.52), kind=kCustom, calls=%fused_computation.30 | custom fusion | flops 65536 | bytes 786944 | tf_op jit(solution)/shard_map/scatter-add | solution.py:75
  318.9 9.5 %scatter_fusion.11 = f32[64,8,128]{0,1,2:T(8,128)S(1)} fusion(f32[64,8,128]{0,1,2:T(8,128)S(1)} %scatter_fusion.10, s32[128]{0:T(128)S(1)} %get-tuple-element.42, f32[128,64,8]{1,2,0:T(8,128)} %fusion.58), kind=kCustom, calls=%fused_computation.31 | custom fusion | flops 65536 | bytes 786944 | tf_op jit(solution)/shard_map/scatter-add | solution.py:75
  336.5 76.1 %psum.30 = f32[8]{0:T(128)S(1)} all-reduce(f32[8]{0:T(128)S(1)} %multiply_reduce_fusion.1), channel_id=1, replica_groups=mesh['dom'=128,'sub'=2] {'dom','sub'}, use_global_device_ids=true, to_apply=%region_19.23 | all-reduce | flops 8 | bytes 64 | tf_op jit(solution)/shard_map/psum | solution.py:69
  427.1 5.3 fusion.2
  453.5 6.8 %scatter_fusion.14 = f32[64,8,128]{0,1,2:T(8,128)} fusion(f32[64,8,128]{0,1,2:T(8,128)} %fusion.85, s32[64]{0:T(128)S(1)} %copy-done.51, f32[64,64,8]{1,2,0:T(8,128)S(1)} %fusion.89), kind=kCustom, calls=%fused_computation.34 | custom fusion | flops 32768 | bytes 393472 | tf_op jit(solution)/shard_map/scatter-add | solution.py:105
  465.7 7.4 %scatter_fusion.15 = f32[64,8,128]{0,1,2:T(8,128)} fusion(f32[64,8,128]{0,1,2:T(8,128)} %scatter_fusion.14, s32[64]{0:T(128)S(1)} %copy-done.53, f32[64,64,8]{1,2,0:T(8,128)} %convolution_bitcast_fusion), kind=kCustom, calls=%fused_computation.35 | custom fusion | flops 32768 | bytes 393472 | tf_op jit(solution)/shard_map/scatter-add | solution.py:108
  474.4 77.8 %psum.31 = f32[8]{0:T(128)S(1)} all-reduce(f32[8]{0:T(128)S(1)} %multiply_reduce_fusion), channel_id=1, replica_groups=mesh['dom'=128,'sub'=2] {'dom','sub'}, use_global_device_ids=true, to_apply=%region_23.27 | all-reduce | flops 8 | bytes 64 | tf_op jit(solution)/shard_map/psum | solution.py:111
  583.3 9.5 %scatter_fusion.16 = f32[64,8,128]{0,1,2:T(8,128)S(1)} fusion(f32[64,8,128]{0,1,2:T(8,128)S(1)} %broadcast.133, s32[128]{0:T(128)S(1)} %copy-done.36, f32[128,64,8]{1,2,0:T(8,128)} %fusion.43), kind=kCustom, calls=%fused_computation.36 | custom fusion | flops 65536 | bytes 786944 | tf_op jit(solution)/shard_map/scatter-add | solution.py:75
  592.8 4.9 scatter_fusion.17
  597.8 4.9 scatter_fusion.18
  602.7 4.9 scatter_fusion.19
  (288 shorter events, 219.8 us)
Async XLA Ops:
  8.6 95.4 %collective-permute-start.1 = (f32[64,8,32]{0,1,2:T(8,128)S(1)}, f32[64,8,32]{0,1,2:T(8,128)S(1)}, u32[]{:S(2)}, u32[]{:S(2)}) collective-permute-start(f32[64,8,32]{0,1,2:T(8,128)S(1)} %get-tuple-element.35), channel_id=1, source_target_pairs={{1,0},{2,1},{3,2},{4,3},{5,4},{6,5},{7,6},{8,7},{9,8},{10,9},{11,1... | collective-permute-start | bytes 196616 | tf_op jit(solution)/shard_map/ppermute | solution.py:17
  13.8 90.3 %collective-permute-start = (f32[64,8,32]{0,1,2:T(8,128)S(1)}, f32[64,8,32]{0,1,2:T(8,128)}, u32[]{:S(2)}, u32[]{:S(2)}) collective-permute-start(f32[64,8,32]{0,1,2:T(8,128)S(1)} %get-tuple-element.34), channel_id=1, source_target_pairs={{0,1},{1,2},{2,3},{3,4},{4,5},{5,6},{6,7},{7,8},{8,9},{9,10},{10,1... | collective-permute-start | bytes 196616 | tf_op jit(solution)/shard_map/ppermute | solution.py:16
  21.9 86.0 %collective-permute-start.2 = (f32[64,8,64]{2,0,1:T(8,128)}, f32[64,8,64]{2,0,1:T(8,128)}, u32[]{:S(2)}, u32[]{:S(2)}) collective-permute-start(f32[64,8,64]{2,0,1:T(8,128)} %fusion.127), channel_id=1, source_target_pairs={{0,128},{1,129},{2,130},{3,131},{4,132},{5,133},{6,134},{7,135},{8... | collective-permute-start | bytes 393224 | tf_op jit(solution)/shard_map/ppermute | solution.py:23
  25.4 37.3 %copy-start.40 = (s32[64]{0:T(128)}, s32[64]{0:T(128)S(1)}, u32[]{:S(2)}) copy-start(s32[64]{0:T(128)S(1)} %compare_select_fusion.8) | copy-start | bytes 772
  26.0 37.3 %copy-start.38 = (s32[64]{0:T(128)}, s32[64]{0:T(128)S(1)}, u32[]{:S(2)}) copy-start(s32[64]{0:T(128)S(1)} %compare_select_fusion.7) | copy-start | bytes 772
  121.0 30.0 %collective-permute-start.4 = (f32[64,8,32]{0,1,2:T(8,128)}, f32[64,8,32]{0,1,2:T(8,128)S(1)}, u32[]{:S(2)}, u32[]{:S(2)}) collective-permute-start(f32[64,8,32]{0,1,2:T(8,128)} %get-tuple-element.33), channel_id=1, source_target_pairs={{1,0},{2,1},{3,2},{4,3},{5,4},{6,5},{7,6},{8,7},{9,8},{10,9},{11,1... | collective-permute-start | bytes 196616 | tf_op jit(solution)/shard_map/ppermute | solution.py:17
  129.5 21.5 %collective-permute-start.3 = (f32[64,8,32]{0,1,2:T(8,128)}, f32[64,8,32]{0,1,2:T(8,128)}, u32[]{:S(2)}, u32[]{:S(2)}) collective-permute-start(f32[64,8,32]{0,1,2:T(8,128)} %get-tuple-element.32), channel_id=1, source_target_pairs={{0,1},{1,2},{2,3},{3,4},{4,5},{5,6},{6,7},{7,8},{8,9},{9,10},{10,1... | collective-permute-start | bytes 196616 | tf_op jit(solution)/shard_map/ppermute | solution.py:16
  133.8 27.3 %collective-permute-start.5 = (f32[64,8,64]{0,1,2:T(8,128)}, f32[64,8,64]{0,1,2:T(8,128)}, u32[]{:S(2)}, u32[]{:S(2)}) collective-permute-start(f32[64,8,64]{0,1,2:T(8,128)} %select_bitcast_fusion.2), channel_id=1, source_target_pairs={{0,128},{1,129},{2,130},{3,131},{4,132},{5,133},{6,134},{7,135},{8... | collective-permute-start | bytes 393224 | tf_op jit(solution)/shard_map/ppermute | solution.py:23
  153.6 21.7 %copy-start.65 = (f32[8]{0:T(128)S(1)}, f32[8]{0:T(128)}, u32[]{:S(2)}) copy-start(f32[8]{0:T(128)} %multiply_reduce_fusion.3) | copy-start | bytes 100
  270.8 15.5 %copy-start.17 = (f32[64,8,128]{0,1,2:T(8,128)S(1)}, f32[64,8,128]{0,1,2:T(8,128)}, u32[]{:S(2)}) copy-start(f32[64,8,128]{0,1,2:T(8,128)} %copy-done.16) | copy-start | bytes 786436
  273.9 54.5 %collective-permute-start.7 = (f32[64,8,32]{0,1,2:T(8,128)}, f32[64,8,32]{0,1,2:T(8,128)}, u32[]{:S(2)}, u32[]{:S(2)}) collective-permute-start(f32[64,8,32]{0,1,2:T(8,128)} %get-tuple-element.31), channel_id=1, source_target_pairs={{1,0},{2,1},{3,2},{4,3},{5,4},{6,5},{7,6},{8,7},{9,8},{10,9},{11,1... | collective-permute-start | bytes 196616 | tf_op jit(solution)/shard_map/ppermute | solution.py:17
  276.5 51.9 %collective-permute-start.6 = (f32[64,8,32]{0,1,2:T(8,128)S(1)}, f32[64,8,32]{0,1,2:T(8,128)}, u32[]{:S(2)}, u32[]{:S(2)}) collective-permute-start(f32[64,8,32]{0,1,2:T(8,128)S(1)} %get-tuple-element.30), channel_id=1, source_target_pairs={{0,1},{1,2},{2,3},{3,4},{4,5},{5,6},{6,7},{7,8},{8,9},{9,10},{10,1... | collective-permute-start | bytes 196616 | tf_op jit(solution)/shard_map/ppermute | solution.py:16
  284.7 15.2 %copy-start.33 = (s32[128]{0:T(128)S(1)}, s32[128]{0:T(128)}, u32[]{:S(2)}) copy-start(s32[128]{0:T(128)} %get-tuple-element.43) | copy-start | bytes 1540
  284.7 47.6 %collective-permute-start.8 = (f32[64,8,64]{2,0,1:T(8,128)}, f32[64,8,64]{2,0,1:T(8,128)}, u32[]{:S(2)}, u32[]{:S(2)}) collective-permute-start(f32[64,8,64]{2,0,1:T(8,128)} %fusion.121), channel_id=1, source_target_pairs={{0,128},{1,129},{2,130},{3,131},{4,132},{5,133},{6,134},{7,135},{8... | collective-permute-start | bytes 393224 | tf_op jit(solution)/shard_map/ppermute | solution.py:23
  439.5 12.2 %collective-permute-start.10 = (f32[64,8,32]{0,1,2:T(8,128)S(1)}, f32[64,8,32]{0,1,2:T(8,128)S(1)}, u32[]{:S(2)}, u32[]{:S(2)}) collective-permute-start(f32[64,8,32]{0,1,2:T(8,128)S(1)} %get-tuple-element.29), channel_id=1, source_target_pairs={{1,0},{2,1},{3,2},{4,3},{5,4},{6,5},{7,6},{8,7},{9,8},{10,9},{11,1... | collective-permute-start | bytes 196616 | tf_op jit(solution)/shard_map/ppermute | solution.py:17
  442.1 9.6 %collective-permute-start.9 = (f32[64,8,32]{0,1,2:T(8,128)S(1)}, f32[64,8,32]{0,1,2:T(8,128)S(1)}, u32[]{:S(2)}, u32[]{:S(2)}) collective-permute-start(f32[64,8,32]{0,1,2:T(8,128)S(1)} %get-tuple-element.28), channel_id=1, source_target_pairs={{0,1},{1,2},{2,3},{3,4},{4,5},{5,6},{6,7},{7,8},{8,9},{9,10},{10,1... | collective-permute-start | bytes 196616 | tf_op jit(solution)/shard_map/ppermute | solution.py:16
  446.0 14.3 %collective-permute-start.11 = (f32[64,8,64]{0,1,2:T(8,128)}, f32[64,8,64]{0,1,2:T(8,128)}, u32[]{:S(2)}, u32[]{:S(2)}) collective-permute-start(f32[64,8,64]{0,1,2:T(8,128)} %select_bitcast_fusion), channel_id=1, source_target_pairs={{0,128},{1,129},{2,130},{3,131},{4,132},{5,133},{6,134},{7,135},{8... | collective-permute-start | bytes 393224 | tf_op jit(solution)/shard_map/ppermute | solution.py:23
  453.5 98.7 %copy-start.18 = (f32[64,8,128]{0,1,2:T(8,128)S(1)}, f32[64,8,128]{0,1,2:T(8,128)}, u32[]{:S(2)}) copy-start(f32[64,8,128]{0,1,2:T(8,128)} %copy-done.16) | copy-start | bytes 786436
  453.5 98.7 %copy-start.63 = (f32[8]{0:T(128)S(1)}, f32[8]{0:T(128)}, u32[]{:S(2)}) copy-start(f32[8]{0:T(128)} %copy-done.62) | copy-start | bytes 100
  569.1 38.6 %collective-permute-start.13 = (f32[64,8,32]{0,1,2:T(8,128)}, f32[64,8,32]{0,1,2:T(8,128)}, u32[]{:S(2)}, u32[]{:S(2)}) collective-permute-start(f32[64,8,32]{0,1,2:T(8,128)} %get-tuple-element.27), channel_id=1, source_target_pairs={{1,0},{2,1},{3,2},{4,3},{5,4},{6,5},{7,6},{8,7},{9,8},{10,9},{11,1... | collective-permute-start | bytes 196616 | tf_op jit(solution)/shard_map/ppermute | solution.py:17
  571.6 36.0 %collective-permute-start.12 = (f32[64,8,32]{0,1,2:T(8,128)S(1)}, f32[64,8,32]{0,1,2:T(8,128)}, u32[]{:S(2)}, u32[]{:S(2)}) collective-permute-start(f32[64,8,32]{0,1,2:T(8,128)S(1)} %get-tuple-element.26), channel_id=1, source_target_pairs={{0,1},{1,2},{2,3},{3,4},{4,5},{5,6},{6,7},{7,8},{8,9},{9,10},{10,1... | collective-permute-start | bytes 196616 | tf_op jit(solution)/shard_map/ppermute | solution.py:16
  577.4 34.0 %collective-permute-start.14 = (f32[64,8,64]{2,0,1:T(8,128)S(1)}, f32[64,8,64]{2,0,1:T(8,128)}, u32[]{:S(2)}, u32[]{:S(2)}) collective-permute-start(f32[64,8,64]{2,0,1:T(8,128)S(1)} %fusion.115), channel_id=1, source_target_pairs={{0,128},{1,129},{2,130},{3,131},{4,132},{5,133},{6,134},{7,135},{8... | collective-permute-start | bytes 393224 | tf_op jit(solution)/shard_map/ppermute | solution.py:23
  582.3 15.4 %copy-start.22 = (f32[128,64,8]{1,2,0:T(8,128)S(1)}, f32[128,64,8]{1,2,0:T(8,128)}, u32[]{:S(2)}) copy-start(f32[128,64,8]{1,2,0:T(8,128)} %fusion.55) | copy-start | bytes 786436
  583.3 19.4 %copy-start.25 = (f32[128,64,8]{1,2,0:T(8,128)S(1)}, f32[128,64,8]{1,2,0:T(8,128)}, u32[]{:S(2)}) copy-start(f32[128,64,8]{1,2,0:T(8,128)} %fusion.61) | copy-start | bytes 786436
  (62 other events, 411.2 us)
where the time goes:
time: 627 us; the launch traced here: 617 us
  blocking collectives  236 us (38%)
  other arithmetic  168 us (27%)
  matrix products  95 us (15%)
  local copies, waits for them, and re-layouts  74.2 us (12%)
  starting transfers between devices  41 us (7%)
    psum x2, blocking collectives, total_squares(): return lax.psum(local_inner(field, field), ('dom', 'sub'))  158 us
    scatter-add x12, other arithmetic, transpose(): result.at[:, :, inner_cols[index]]  100 us
    dot_general x30, matrix products, tile_apply(): jnp.einsum(form, tiles.astype(jnp.float32), vectors, precision=lax.Precis...  92 us
    psum x1, blocking collectives, shards(): lax.psum(local_inner(forward_result, forward_result), ('dom', 'sub'))  77.8 us
    unnamed x152, local copies, waits for them, and re-layouts  28.3 us
    ppermute x5, starting transfers between devices, with_halo(): after = lax.ppermute(initial, axis, down)  21.3 us
    gather x8, local copies, waits for them, and re-layouts, shards(): gathered = jnp.take(direction, inner_cols[forward_index], axis=2)  17.3 us
    scatter-add x2, other arithmetic, shards(): forward_result.at[:, :, contact_rows]  14.9 us
  transfers between devices with their start and end apart: 15, of which 0 were waited for; matrix products, arithmetic and copies ran while one was open for 35% of the time, Pallas kernels for 0%

commit v1 on v0

v1 whole, which is shorter than its diff:
```python
import functools

import jax
import jax.numpy as jnp
from jax import lax
from jax.experimental import pallas as pl
from jax.experimental.pallas import tpu as pltpu
from jax.sharding import PartitionSpec as P

F32 = jnp.float32
BF16 = jnp.bfloat16
APPS = 5
MESH = pl.DeviceIdType.MESH
NT = (((1,), (1,)), ((), ()))


def stage_sizes(devices):
    bits = devices.bit_length() - 1
    first = min(3, bits - 2)
    second = min(3, bits - first - 1)
    return (1 << first, 1 << second, 1 << (bits - first - second))


def low_half(shape):
    return lax.broadcasted_iota(jnp.int32, shape, 1) < 64


def swap(x):
    return pltpu.roll(x, 64, 1)


def pair(x, y):
    low = low_half(x.shape)
    return jnp.where(low, x, swap(y)), jnp.where(low, swap(x), y)


def split(x):
    high = x.astype(BF16)
    return high, (x - high.astype(F32)).astype(BF16)


def split_wide(x):
    high = x.astype(BF16).astype(F32)
    return high, x - high


def dot(a, b):
    return jnp.dot(a, b, preferred_element_type=F32)


def dot_nt(a, b):
    return lax.dot_general(a, b, NT, preferred_element_type=F32)


def split_dot(product, a, b):
    rows = a.shape[0]
    out = product(jnp.concatenate(split(a), axis=0), b)
    return out[:rows] + out[rows:]


def block8(ref, index):
    return ref[pl.ds(pl.multiple_of(index * 8, 8), 8), :]


def put8(ref, index, value):
    ref[pl.ds(pl.multiple_of(index * 8, 8), 8), :] = value


def every8(first, count):
    return pl.ds(first, count, stride=8)


def kernel(
    devices,
    cols_s,
    frows_s,
    crows_s,
    counts_s,
    rhs,
    tiles,
    cols_v,
    send_v,
    rows_v,
    pair_v,
    ftiles,
    ctiles,
    adjoint,
    residual,
    normal,
    wf0,
    wf1,
    w,
    ef,
    e,
    ohk,
    ohs,
    ohst,
    ohr,
    p01,
    p23,
    z0,
    q,
    t,
    f0,
    fw,
    fs,
    u,
    xf,
    ps,
    uo,
    sbuf,
    rbuf,
    arsend,
    arrecv,
    xsend,
    xrecv,
    asend,
    arecv,
):
    me = lax.axis_index("dom") * 2 + lax.axis_index("sub")
    sizes = stage_sizes(devices)

    def place(index):
        return (index // 2, lax.rem(index, 2))

    lower = lax.rem(me + devices - 1, devices)
    upper = lax.rem(me + 1, devices)
    partner = lax.rem(me + devices // 2, devices)

    def group_peers(stage):
        stride = 1
        for size in sizes[:stage]:
            stride *= size
        size = sizes[stage]
        mine = lax.rem(me // stride, size)
        return [me + (lax.rem(mine + i, size) - mine) * stride for i in range(1, size)]

    peers = [group_peers(stage) for stage in range(3)]
    everyone = [lower, upper, partner] + peers[0] + peers[1] + peers[2]

    barrier = pltpu.get_barrier_semaphore()
    for other in everyone:
        pl.semaphore_signal(barrier, inc=1, device_id=place(other), device_id_type=MESH)

    row_id = lax.broadcasted_iota(jnp.int32, (128, 128), 0)
    lane_id = lax.broadcasted_iota(jnp.int32, (128, 128), 1)
    for k in range(4):
        ohk[:, k * 128 : (k + 1) * 128] = jnp.where(
            cols_v[k : k + 1, :] == row_id, 1.0, 0.0
        ).astype(BF16)
    picks = jnp.where(send_v[...] == row_id, 1.0, 0.0)
    ohs[...] = picks.astype(BF16)
    ohst[...] = picks.T.astype(BF16)
    ohr[...] = jnp.where(rows_v[...] == row_id, 1.0, 0.0).astype(BF16)
    eye = jnp.where(row_id == lane_id, 1.0, 0.0).astype(BF16)

    def prepare(a, carry):
        for half, out in ((0, wf0), (1, wf1)):
            x = tiles[2 * half : 2 * half + 2, a].reshape(128, 128)
            x = dot_nt(eye, x)
            out[pl.ds(a, 64, stride=128), :] = x[:64]
            out[pl.ds(64 + a, 64, stride=128), :] = x[64:]
        return carry

    lax.fori_loop(0, 64, prepare, 0, unroll=2)

    def pack(i, carry):
        at = pl.ds(pl.multiple_of(i * 128, 128), 128)
        w[at, 0:128] = wf0[at, :].astype(BF16)
        w[at, 128:256] = wf1[at, :].astype(BF16)
        return carry

    lax.fori_loop(0, 64, pack, 0, unroll=2)

    slot = lax.broadcasted_iota(jnp.int32, (64, 64), 0)
    other_slot = lax.broadcasted_iota(jnp.int32, (64, 64), 1)
    side_a = (slot < 32) & (slot < counts_s[0, 0])
    side_b = (slot >= 32) & (slot - 32 < counts_s[0, 1])
    face_pick = jnp.where((slot == other_slot) & (side_a | side_b), 1.0, 0.0)
    contact_pick = jnp.where(pair_v[...] == slot, 1.0, 0.0)
    slot_pick = jnp.concatenate([face_pick, contact_pick], axis=0).astype(BF16)

    def prepare_slots(a, carry):
        x = jnp.concatenate([ftiles[a], ctiles[a]], axis=0)
        x = dot_nt(slot_pick, x)
        x = jnp.where(low_half((64, 128)), x[:64], x[64:])
        ef[pl.ds(a, 32, stride=128), :] = x[:32]
        ef[pl.ds(64 + a, 32, stride=128), :] = x[32:]
        return carry

    lax.fori_loop(0, 64, prepare_slots, 0, unroll=2)

    def pack_slots(i, carry):
        at = pl.ds(pl.multiple_of(i * 128, 128), 128)
        e[at, :] = ef[at, :].astype(BF16)
        return carry

    lax.fori_loop(0, 32, pack_slots, 0, unroll=2)

    def tile_at(ref, index):
        return ref[pl.ds(pl.multiple_of(index * 128, 128), 128), :]

    low8 = low_half((8, 128))
    zero8 = jnp.zeros((8, 128), F32)

    def spread(field):
        x = field[...]
        y = swap(x)
        low = low_half(x.shape)
        u[0:64] = jnp.where(low, x, y).reshape(64, 8, 128)
        u[64:128] = jnp.where(low, y, x).reshape(64, 8, 128)

    for n in range(8):
        x = rhs[every8(n, 64), :]
        x = jnp.concatenate([x, x], axis=0).T
        u[:, n, :] = x
        f0[every8(n, 64), :] = jnp.where(low_half((64, 128)), x[:64], x[64:])

    pl.semaphore_wait(barrier, len(everyone))

    def exchange(app):
        copies = []
        for index, (other, start, stop, to) in enumerate(
            ((lower, 0, 32, 32), (upper, 32, 64, 0), (partner, 64, 128, 64))
        ):
            copy = pltpu.make_async_remote_copy(
                src_ref=sbuf.at[app, :, pl.ds(start, stop - start), :],
                dst_ref=rbuf.at[app, :, pl.ds(to, stop - start), :],
                send_sem=xsend.at[app, index],
                recv_sem=xrecv.at[app, index],
                device_id=place(other),
                device_id_type=MESH,
            )
            copy.start()
            copies.append(copy)
        return copies

    def reduce_start(which, stage, value):
        arsend[which, stage] = value
        first = sum(size - 1 for size in sizes[:stage])
        copies = []
        for index, other in enumerate(peers[stage]):
            copy = pltpu.make_async_remote_copy(
                src_ref=arsend.at[which, stage],
                dst_ref=arrecv.at[which, first + index],
                send_sem=asend.at[which, first + index],
                recv_sem=arecv.at[which, first + index],
                device_id=place(other),
                device_id_type=MESH,
            )
            copy.start()
            copies.append(copy)
        return copies

    def reduce_end(which, stage, copies):
        for copy in copies:
            copy.wait()
        total = arsend[which, stage]
        first = sum(size - 1 for size in sizes[:stage])
        for index in range(len(copies)):
            total = total + arrecv[which, first + index]
        return total

    def transpose_slots(app):
        def body(sp, carry):
            parts = [
                jnp.where(low8, u[frows_s[sp]], zero8),
                jnp.where(low8, zero8, u[frows_s[32 + sp]]),
                jnp.where(low8, u[crows_s[sp]], zero8),
                jnp.where(low8, zero8, u[crows_s[32 + sp]]),
            ]
            out = split_dot(dot, jnp.concatenate(parts, axis=0), tile_at(e, sp))
            put8(ps, sp, jnp.where(low8, out[0:8], out[16:24]))
            put8(ps, 32 + sp, jnp.where(low8, out[8:16], out[24:32]))
            return carry

        lax.fori_loop(0, 32, body, 0, unroll=4)
        for np in range(4):
            face, contact = pair(ps[every8(2 * np, 64), :], ps[every8(2 * np + 1, 64), :])
            sbuf[app, np, 0:64] = face
            sbuf[app, np, 64:128] = contact
        return exchange(app)

    def transpose_inner(field):
        def body(jp, carry):
            high, rest = split_wide(block8(field, jp))
            parts = [
                jnp.where(low8, high, zero8),
                jnp.where(low8, rest, zero8),
                jnp.where(low8, zero8, high),
                jnp.where(low8, zero8, rest),
            ]
            out = dot(jnp.concatenate(parts, axis=0).astype(BF16), tile_at(w, jp))
            x = out[0:8] + out[8:16]
            y = out[16:24] + out[24:32]
            put8(p01, jp, x[:, :128])
            put8(p23, jp, x[:, 128:])
            put8(p01, 64 + jp, y[:, :128])
            put8(p23, 64 + jp, y[:, 128:])
            return carry

        lax.fori_loop(0, 64, body, 0, unroll=4)

    def transpose_end(app, copies, result, send_app):
        for copy in copies:
            copy.wait()
        low = low_half((128, 128))
        for np in range(4):
            k0, k1 = pair(p01[every8(2 * np, 128), :], p01[every8(2 * np + 1, 128), :])
            k2, k3 = pair(p23[every8(2 * np, 128), :], p23[every8(2 * np + 1, 128), :])
            high, rest = split(jnp.concatenate([k0, k1, k2, k3], axis=0))
            z = dot(ohk[...], high) + dot(ohk[...], rest)
            high, rest = split(rbuf[app, np])
            z = z + (dot(ohs[...], high) + dot(ohs[...], rest))
            if send_app is not None:
                high, rest = split(z)
                sbuf[send_app, np] = dot(ohst[...], high) + dot(ohst[...], rest)
            other = swap(z)
            result[:, 2 * np, :] = jnp.where(low, z, other)
            result[:, 2 * np + 1, :] = jnp.where(low, other, z)
        if send_app is not None:
            return exchange(send_app)

    def forward_inner(field, result):
        def body(jp, carry):
            parts = []
            for j2 in range(2):
                j = j2 * 64 + jp
                v = [field[cols_s[k, j]] for k in range(4)]
                x = jnp.concatenate(
                    [jnp.where(low8, v[0], v[1]), jnp.where(low8, v[2], v[3])], axis=1
                )
                parts += list(split_wide(x))
            out = dot_nt(jnp.concatenate(parts, axis=0).astype(BF16), tile_at(w, jp))
            put8(result, jp, jnp.where(low8, out[0:8] + out[8:16], out[16:24] + out[24:32]))
            return carry

        lax.fori_loop(0, 64, body, 0, unroll=4)

    def forward_end(app, copies, result):
        for copy in copies:
            copy.wait()
        low = low_half((64, 128))
        for np in range(4):
            x = rbuf[app, np]
            face, contact = x[:64], x[64:]
            xf[every8(2 * np, 64), :] = jnp.where(low, face, 0.0)
            xf[every8(2 * np + 1, 64), :] = jnp.where(low, swap(face), 0.0)
            xf[every8(512 + 2 * np, 64), :] = jnp.where(low, 0.0, swap(contact))
            xf[every8(512 + 2 * np + 1, 64), :] = jnp.where(low, 0.0, contact)

        def body(sp, carry):
            parts = [block8(xf, sp + 32 * i) for i in range(4)]
            out = split_dot(dot_nt, jnp.concatenate(parts, axis=0), tile_at(e, sp))
            put8(uo, sp, jnp.where(low8, out[0:8], out[8:16]))
            put8(uo, 32 + sp, jnp.where(low8, out[16:24], out[24:32]))
            return carry

        lax.fori_loop(0, 32, body, 0, unroll=4)
        for np in range(4):
            s0, s1 = pair(uo[every8(2 * np, 64), :], uo[every8(2 * np + 1, 64), :])
            high, rest = split(jnp.concatenate([s0, s1], axis=0))
            y = dot(ohr[...], high) + dot(ohr[...], rest)
            n0, n1 = pair(y[:64], y[64:])
            result[every8(2 * np, 64), :] = result[every8(2 * np, 64), :] + n0
            result[every8(2 * np + 1, 64), :] = result[every8(2 * np + 1, 64), :] + n1

    def total(x):
        x = jnp.sum(x.reshape(-1, 8, 128), axis=0)
        return jnp.broadcast_to(jnp.sum(x, axis=1, keepdims=True), (8, 128))

    lane8 = lax.broadcasted_iota(jnp.int32, (8, 128), 1)

    def column(x, index):
        return jnp.broadcast_to(x[:, index : index + 1], (8, 128))

    def each(x, rows):
        return jnp.broadcast_to(x[None], (rows // 8, 8, 128)).reshape(rows, 128)

    copies = transpose_slots(0)
    transpose_inner(f0)
    copies = transpose_end(0, copies, z0, 1)
    forward_inner(z0, fw)
    zz = total(z0[...] * z0[...]) * 0.5
    forward_end(1, copies, fw)
    ww = total(fw[...] * fw[...])
    going = reduce_start(0, 0, jnp.where(lane8 < 64, zz, ww))
    spread(fw)
    copies = transpose_slots(2)
    going = reduce_start(0, 1, reduce_end(0, 0, going))
    transpose_inner(fw)
    going = reduce_start(0, 2, reduce_end(0, 1, going))
    copies = transpose_end(2, copies, q, 3)
    forward_inner(q, fs)
    sums = reduce_end(0, 2, going)
    zz0 = column(sums, 0)
    ww0 = column(sums, 64)
    alpha0 = zz0 / ww0
    forward_end(3, copies, fs)
    fs[...] = fw[...] - each(alpha0, 512) * fs[...]
    spread(fs)
    copies = transpose_slots(4)
    z1 = z0[...] - alpha0[None] * q[...]
    s1 = fs[...]
    zz = total(z1 * z1) * 0.5
    ss = total(s1 * s1)
    sw = total(s1 * fw[...])
    going = reduce_start(1, 0, jnp.where(lane8 < 32, zz, jnp.where(lane8 < 64, ss, sw)))
    transpose_inner(fs)
    going = reduce_start(1, 1, reduce_end(1, 0, going))
    transpose_end(4, copies, t, None)
    going = reduce_start(1, 2, reduce_end(1, 1, going))
    sums = reduce_end(1, 2, going)
    zz1 = column(sums, 0)
    beta = zz1 / zz0
    ww1 = column(sums, 32) + beta * (2.0 * column(sums, 64) + beta * ww0)
    alpha1 = zz1 / ww1

    a0, a1, b = (x[None] for x in (alpha0, alpha1, beta))
    z1 = z0[...] - a0 * q[...]
    t[...] = z1 - a1 * (t[...] + b * q[...])
    z0[...] = a0 * z0[...] + a1 * (z1 + b * z0[...])
    a0, a1, b = (each(x, 512) for x in (alpha0, alpha1, beta))
    f0[...] = f0[...] - a0 * fw[...] - a1 * (fs[...] + b * fw[...])

    low = low_half((128, 128))
    for np in range(4):
        for source, out in ((z0, adjoint), (t, normal)):
            x = jnp.where(low, source[:, 2 * np, :], source[:, 2 * np + 1, :]).T
            out[every8(2 * np, 64), :] = x[:64]
            out[every8(2 * np + 1, 64), :] = x[64:]
        top, bottom = pair(f0[every8(2 * np, 64), :], f0[every8(2 * np + 1, 64), :])
        x = jnp.concatenate([top, bottom], axis=0).T
        residual[every8(2 * np, 64), :] = x[:64]
        residual[every8(2 * np + 1, 64), :] = x[64:]


def shards(
    devices,
    rhs,
    inner_tiles,
    inner_cols,
    send_blocks,
    face_rows,
    face_counts,
    face_tiles,
    contact_send,
    contact_rows,
    contact_pair,
    contact_tiles,
):
    slot = jnp.arange(64, dtype=jnp.int32)
    paired_rows = jnp.sum(
        jnp.where(contact_pair[0][:, None] == slot[None, :], contact_rows[:, None], 0), axis=0
    )
    sends = jnp.concatenate([send_blocks, contact_send])[None]
    rows = jnp.concatenate(
        [face_rows[:32], paired_rows[:32], face_rows[32:], paired_rows[32:]]
    )[None]
    smem = pl.BlockSpec(memory_space=pltpu.SMEM)
    vmem = pl.BlockSpec(memory_space=pltpu.VMEM)
    copies = sum(size - 1 for size in stage_sizes(devices))
    out = jax.ShapeDtypeStruct((512, 128), F32)
    outs = pl.pallas_call(
        functools.partial(kernel, devices),
        out_shape=[out] * 3,
        in_specs=[smem] * 4 + [vmem] * 8,
        out_specs=[vmem] * 3,
        scratch_shapes=[
            pltpu.VMEM((8192, 128), F32),
            pltpu.VMEM((8192, 128), F32),
            pltpu.VMEM((8192, 256), BF16),
            pltpu.VMEM((4096, 128), F32),
            pltpu.VMEM((4096, 128), BF16),
            pltpu.VMEM((128, 512), BF16),
            pltpu.VMEM((128, 128), BF16),
            pltpu.VMEM((128, 128), BF16),
            pltpu.VMEM((128, 128), BF16),
            pltpu.VMEM((1024, 128), F32),
            pltpu.VMEM((1024, 128), F32),
            pltpu.VMEM((128, 8, 128), F32),
            pltpu.VMEM((128, 8, 128), F32),
            pltpu.VMEM((128, 8, 128), F32),
            pltpu.VMEM((512, 128), F32),
            pltpu.VMEM((512, 128), F32),
            pltpu.VMEM((512, 128), F32),
            pltpu.VMEM((128, 8, 128), F32),
            pltpu.VMEM((1024, 128), F32),
            pltpu.VMEM((512, 128), F32),
            pltpu.VMEM((512, 128), F32),
            pltpu.VMEM((APPS, 4, 128, 128), F32),
            pltpu.VMEM((APPS, 4, 128, 128), F32),
            pltpu.VMEM((2, 3, 8, 128), F32),
            pltpu.VMEM((2, copies, 8, 128), F32),
            pltpu.SemaphoreType.DMA((APPS, 3)),
            pltpu.SemaphoreType.DMA((APPS, 3)),
            pltpu.SemaphoreType.DMA((2, copies)),
            pltpu.SemaphoreType.DMA((2, copies)),
        ],
        compiler_params=pltpu.CompilerParams(
            collective_id=0, has_side_effects=True, vmem_limit_bytes=56 * 1024 * 1024
        ),
    )(
        inner_cols,
        face_rows,
        paired_rows,
        face_counts,
        rhs.reshape(512, 128),
        inner_tiles,
        inner_cols,
        sends,
        rows,
        contact_pair,
        face_tiles,
        contact_tiles,
    )
    return tuple(x.reshape(64, 8, 128) for x in outs)


def solution(mesh):
    both = ("dom", "sub")
    field = P(None, None, both)
    devices = 1
    for axis in both:
        devices *= mesh.shape[axis]
    return jax.shard_map(
        functools.partial(shards, devices),
        mesh=mesh,
        in_specs=(
            field,
            P(None, None, None, both),
            P(None, both),
            P(both),
            P(both),
            P(both, None),
            field,
            P(both),
            P(both),
            P(both, None),
            field,
        ),
        out_specs=(field,) * 3,
        check_vma=False,
    )
```

time: 627 us -> 89 us (0.14); the launches traced: 617 us -> 88.3 us
  blocking collectives: 236 us -> 0 us
  other arithmetic: 168 us -> 2.62 us
  matrix products: 95 us -> 0 us
  Pallas kernels: 0 us -> 79.3 us
  local copies, waits for them, and re-layouts: 74.2 us -> 5.81 us
  starting transfers between devices: 41 us -> 0 us
    psum x3 -> x0, blocking collectives: 236 us -> none  [the longest x2 158 us: total_squares(): return lax.psum(local_inner(field, field), ('dom', 'sub'))]
    scatter-add x22 -> x0, other arithmetic: 147 us -> none  [the longest x12 100 us: transpose(): result.at[:, :, inner_cols[index]]]
    dot_general x33 -> x0, matrix products: 95 us -> none  [the longest x30 92 us: tile_apply(): jnp.einsum(form, tiles.astype(jnp.float32), vectors, precision=lax.Precis...]
    pallas_call x0 -> x1, Pallas kernels: none -> 79.3 us  [shards(): pl.pallas_call(functools.partial(kernel, devices), out_shape=[out] * 3, i...]
    ppermute x15 -> x0, starting transfers between devices: 41 us -> none  [the longest x5 21.3 us: with_halo(): after = lax.ppermute(initial, axis, down)]
    gather x20 -> x0, local copies, waits for them, and re-layouts: 34.1 us -> none  [the longest x8 17.3 us: shards(): gathered = jnp.take(direction, inner_cols[forward_index], axis=2)]
    unnamed x152 -> x5, local copies, waits for them, and re-layouts: 28.3 us -> 5.01 us
  transfers between devices with their start and end apart: 15 -> 0, of which waited for: 0 -> 0; matrix products, arithmetic and copies ran while one was open for 35% -> 0% of each run, Pallas kernels for 0% -> 0%
where the time goes in v1:
time: 89 us; the launch traced here: 88.3 us
  Pallas kernels  79.3 us (89%)
  local copies, waits for them, and re-layouts  5.81 us (7%)
  other arithmetic  2.62 us (3%)
    pallas_call x1, Pallas kernels, shards(): pl.pallas_call(functools.partial(kernel, devices), out_shape=[out] * 3, i...  79.3 us
    unnamed x5, local copies, waits for them, and re-layouts  5.01 us

profile of v1, /device:TPU:1, one launch (start us, length us, event | category | flops | bytes accessed | tf_op | source)
XLA Modules:
  0.0 88.3 jit_solution(16304758536466493891)
XLA Ops:
  0.6 0.8 select_reduce_fusion.crows_s
  1.4 0.0 copy-start
  1.4 1.3 %add_bitcast_fusion.send_v = s32[1,128]{1,0:T(1,128)} fusion(s32[64]{0:T(128)} %param.18, s32[64]{0:T(128)} %param.14), kind=kLoop, calls=%fused_computation.2 | loop fusion | flops 128 | bytes 1024 | tf_op jit(solution)/shard_map/broadcast_in_dim | solution.py:456
  2.7 0.8 fusion
  3.5 0.6 add_bitcast_fusion.1.rows_v
  4.1 0.0 copy-done
  4.1 79.3 %shard_map.130 = (f32[512,128]{1,0:T(8,128)}, f32[512,128]{1,0:T(8,128)}, f32[512,128]{1,0:T(8,128)}) custom-call(s32[4,128]{1,0:T(4,128)} %cols_v.1, s32[64]{0:T(128)} %frows_s.1, s32[64]{0:T(128)} %copy-done, s32[1,2]{1,0:T(1,128)} %counts_s.1, f32[512,128]{1,0:T(8,128)} %bitcast.9, bf16[4,64,64,128]{3,2,1,0:T(8,128)(2,1)} %tiles.1, s32[4,128]{1,0:T(4,128)} %cols_v.1, ...), custom_call_target="tpu_custom_call" | custom-call | tf_op jit(solution)/shard_map/pallas_call | solution.py:464
  83.3 1.7 %copy.17 = f32[64,8,128]{2,1,0:T(8,128)} copy(f32[64,8,128]{2,1,0:T(8,128)} %bitcast.12) | data formatting | bytes 524288
  85.0 1.7 %copy.18 = f32[64,8,128]{2,1,0:T(8,128)} copy(f32[64,8,128]{2,1,0:T(8,128)} %bitcast.11) | data formatting | bytes 524288
  86.7 1.7 %copy.19 = f32[64,8,128]{2,1,0:T(8,128)} copy(f32[64,8,128]{2,1,0:T(8,128)} %bitcast.10) | data formatting | bytes 524288
Async XLA Ops:
  1.4 2.7 %copy-start = (s32[64]{0:T(128)}, s32[64]{0:T(128)S(1)}, u32[]{:S(2)}) copy-start(s32[64]{0:T(128)S(1)} %select_reduce_fusion.crows_s) | copy-start | bytes 772

commit v2 on v1

--- a/solution.py
+++ b/solution.py
@@ -77,16 +77,21 @@
     crows_s,
     counts_s,
     rhs,
-    tiles,
     cols_v,
     send_v,
-    rows_v,
+    csend_v,
+    frows_v,
+    crows_v,
     pair_v,
-    ftiles,
-    ctiles,
+    tiles_h,
+    ftiles_h,
+    ctiles_h,
     adjoint,
     residual,
     normal,
+    tiles,
+    ftiles,
+    ctiles,
     wf0,
     wf1,
     w,
@@ -98,6 +103,7 @@
     ohr,
     p01,
     p23,
+    zs,
     z0,
     q,
     t,
@@ -116,7 +122,16 @@
     xrecv,
     asend,
     arecv,
+    fetched,
 ):
+    fetches = [
+        pltpu.make_async_copy(source, target, fetched.at[index])
+        for index, (source, target) in enumerate(
+            ((ftiles_h, ftiles), (ctiles_h, ctiles), (tiles_h, tiles))
+        )
+    ]
+    for fetch in fetches:
+        fetch.start()
     me = lax.axis_index("dom") * 2 + lax.axis_index("sub")
     sizes = stage_sizes(devices)
 
@@ -144,25 +159,30 @@
 
     row_id = lax.broadcasted_iota(jnp.int32, (128, 128), 0)
     lane_id = lax.broadcasted_iota(jnp.int32, (128, 128), 1)
-    for k in range(4):
-        ohk[:, k * 128 : (k + 1) * 128] = jnp.where(
-            cols_v[k : k + 1, :] == row_id, 1.0, 0.0
-        ).astype(BF16)
-    picks = jnp.where(send_v[...] == row_id, 1.0, 0.0)
-    ohs[...] = picks.astype(BF16)
-    ohst[...] = picks.T.astype(BF16)
-    ohr[...] = jnp.where(rows_v[...] == row_id, 1.0, 0.0).astype(BF16)
+    for half in range(2):
+        for k in range(4):
+            at = half * 512 + k * 128
+            ohk[:, at : at + 128] = jnp.where(cols_v[k : k + 1, :] == row_id, 1.0, 0.0).astype(BF16)
+    picks = jnp.concatenate([send_v[...], csend_v[...]], axis=1) == row_id
+    picks = jnp.where(picks, 1.0, 0.0)
+    ohs[...] = jnp.concatenate([picks.astype(BF16)] * 2, axis=1)
+    picks = picks.T.astype(BF16)
+    ohst[...] = jnp.concatenate([picks] * 2, axis=1)
+    picks = jnp.concatenate([frows_v[...], crows_v[...]], axis=1) == row_id
+    picks = jnp.where(picks, 1.0, 0.0).astype(BF16)
+    ohr[...] = jnp.concatenate([picks] * 2, axis=1)
     eye = jnp.where(row_id == lane_id, 1.0, 0.0).astype(BF16)
 
     def prepare(a, carry):
         for half, out in ((0, wf0), (1, wf1)):
             x = tiles[2 * half : 2 * half + 2, a].reshape(128, 128)
-            x = dot_nt(eye, x)
+            x = turned(half, x)
             out[pl.ds(a, 64, stride=128), :] = x[:64]
             out[pl.ds(64 + a, 64, stride=128), :] = x[64:]
         return carry
 
-    lax.fori_loop(0, 64, prepare, 0, unroll=2)
+    def turned(half, x):
+        return x.astype(F32).T if half else dot_nt(eye, x)
 
     def pack(i, carry):
         at = pl.ds(pl.multiple_of(i * 128, 128), 128)
@@ -170,7 +190,16 @@
         w[at, 128:256] = wf1[at, :].astype(BF16)
         return carry
 
-    lax.fori_loop(0, 64, pack, 0, unroll=2)
+    def prepare_inner():
+        fetches[2].wait()
+        lax.fori_loop(0, 64, prepare, 0, unroll=8)
+        lax.fori_loop(0, 64, pack, 0, unroll=4)
+
+    for n in range(8):
+        x = rhs[every8(n, 64), :]
+        x = jnp.concatenate([x, x], axis=0).T
+        u[:, n, :] = x
+        f0[every8(n, 64), :] = jnp.where(low_half((64, 128)), x[:64], x[64:])
 
     slot = lax.broadcasted_iota(jnp.int32, (64, 64), 0)
     other_slot = lax.broadcasted_iota(jnp.int32, (64, 64), 1)
@@ -180,22 +209,29 @@
     contact_pick = jnp.where(pair_v[...] == slot, 1.0, 0.0)
     slot_pick = jnp.concatenate([face_pick, contact_pick], axis=0).astype(BF16)
 
-    def prepare_slots(a, carry):
-        x = jnp.concatenate([ftiles[a], ctiles[a]], axis=0)
-        x = dot_nt(slot_pick, x)
-        x = jnp.where(low_half((64, 128)), x[:64], x[64:])
-        ef[pl.ds(a, 32, stride=128), :] = x[:32]
-        ef[pl.ds(64 + a, 32, stride=128), :] = x[32:]
+    def prepare_slots(i, carry):
+        parts = []
+        for n in range(4):
+            parts += [ftiles[4 * i + n], ctiles[4 * i + n]]
+        x = dot_nt(slot_pick, jnp.concatenate(parts, axis=0))
+        for n in range(4):
+            a = 4 * i + n
+            y = x[:, 128 * n : 128 * n + 128]
+            y = jnp.where(low_half((64, 128)), y[:64], y[64:])
+            ef[pl.ds(a, 32, stride=128), :] = y[:32]
+            ef[pl.ds(64 + a, 32, stride=128), :] = y[32:]
         return carry
 
-    lax.fori_loop(0, 64, prepare_slots, 0, unroll=2)
+    for fetch in fetches[:2]:
+        fetch.wait()
+    lax.fori_loop(0, 16, prepare_slots, 0, unroll=2)
 
     def pack_slots(i, carry):
         at = pl.ds(pl.multiple_of(i * 128, 128), 128)
         e[at, :] = ef[at, :].astype(BF16)
         return carry
 
-    lax.fori_loop(0, 32, pack_slots, 0, unroll=2)
+    lax.fori_loop(0, 32, pack_slots, 0, unroll=4)
 
     def tile_at(ref, index):
         return ref[pl.ds(pl.multiple_of(index * 128, 128), 128), :]
@@ -209,12 +245,6 @@
         low = low_half(x.shape)
         u[0:64] = jnp.where(low, x, y).reshape(64, 8, 128)
         u[64:128] = jnp.where(low, y, x).reshape(64, 8, 128)
-
-    for n in range(8):
-        x = rhs[every8(n, 64), :]
-        x = jnp.concatenate([x, x], axis=0).T
-        u[:, n, :] = x
-        f0[every8(n, 64), :] = jnp.where(low_half((64, 128)), x[:64], x[64:])
 
     pl.semaphore_wait(barrier, len(everyone))
 
@@ -274,7 +304,7 @@
             put8(ps, 32 + sp, jnp.where(low8, out[8:16], out[24:32]))
             return carry
 
-        lax.fori_loop(0, 32, body, 0, unroll=4)
+        lax.fori_loop(0, 32, body, 0, unroll=8)
         for np in range(4):
             face, contact = pair(ps[every8(2 * np, 64), :], ps[every8(2 * np + 1, 64), :])
             sbuf[app, np, 0:64] = face
@@ -299,27 +329,34 @@
             put8(p23, 64 + jp, y[:, 128:])
             return carry
 
-        lax.fori_loop(0, 64, body, 0, unroll=4)
+        lax.fori_loop(0, 64, body, 0, unroll=8)
+
+    def halves(parts):
+        x = jnp.concatenate(parts, axis=1)
+        return jnp.concatenate(split(x), axis=0)
 
     def transpose_end(app, copies, result, send_app):
+        parts = []
+        for np in range(4):
+            k0, k1 = pair(p01[every8(2 * np, 128), :], p01[every8(2 * np + 1, 128), :])
+            k2, k3 = pair(p23[every8(2 * np, 128), :], p23[every8(2 * np + 1, 128), :])
+            parts.append(jnp.concatenate([k0, k1, k2, k3], axis=0))
+        zs[...] = dot(ohk[...], halves(parts))
         for copy in copies:
             copy.wait()
         low = low_half((128, 128))
-        for np in range(4):
-            k0, k1 = pair(p01[every8(2 * np, 128), :], p01[every8(2 * np + 1, 128), :])
-            k2, k3 = pair(p23[every8(2 * np, 128), :], p23[every8(2 * np + 1, 128), :])
-            high, rest = split(jnp.concatenate([k0, k1, k2, k3], axis=0))
-            z = dot(ohk[...], high) + dot(ohk[...], rest)
-            high, rest = split(rbuf[app, np])
-            z = z + (dot(ohs[...], high) + dot(ohs[...], rest))
-            if send_app is not None:
-                high, rest = split(z)
-                sbuf[send_app, np] = dot(ohst[...], high) + dot(ohst[...], rest)
-            other = swap(z)
-            result[:, 2 * np, :] = jnp.where(low, z, other)
-            result[:, 2 * np + 1, :] = jnp.where(low, other, z)
+        z = zs[...] + dot(ohs[...], halves([rbuf[app, np] for np in range(4)]))
         if send_app is not None:
-            return exchange(send_app)
+            x = dot(ohst[...], jnp.concatenate(split(z), axis=0))
+            for np in range(4):
+                sbuf[send_app, np] = x[:, 128 * np : 128 * np + 128]
+            copies = exchange(send_app)
+        for np in range(4):
+            x = z[:, 128 * np : 128 * np + 128]
+            other = swap(x)
+            result[:, 2 * np, :] = jnp.where(low, x, other)
+            result[:, 2 * np + 1, :] = jnp.where(low, other, x)
+        return copies
 
     def forward_inner(field, result):
         def body(jp, carry):
@@ -335,7 +372,7 @@
             put8(result, jp, jnp.where(low8, out[0:8] + out[8:16], out[16:24] + out[24:32]))
             return carry
 
-        lax.fori_loop(0, 64, body, 0, unroll=4)
+        lax.fori_loop(0, 64, body, 0, unroll=8)
 
     def forward_end(app, copies, result):
         for copy in copies:
@@ -356,14 +393,19 @@
             put8(uo, 32 + sp, jnp.where(low8, out[16:24], out[24:32]))
             return carry
 
-        lax.fori_loop(0, 32, body, 0, unroll=4)
+        lax.fori_loop(0, 32, body, 0, unroll=8)
+        parts = []
         for np in range(4):
             s0, s1 = pair(uo[every8(2 * np, 64), :], uo[every8(2 * np + 1, 64), :])
-            high, rest = split(jnp.concatenate([s0, s1], axis=0))
-            y = dot(ohr[...], high) + dot(ohr[...], rest)
-            n0, n1 = pair(y[:64], y[64:])
-            result[every8(2 * np, 64), :] = result[every8(2 * np, 64), :] + n0
-            result[every8(2 * np + 1, 64), :] = result[every8(2 * np + 1, 64), :] + n1
+            parts.append(jnp.concatenate([s0[:32], s1[:32], s0[32:], s1[32:]], axis=0))
+        y = dot(ohr[...], halves(parts))
+        sums = []
+        for np in range(4):
+            x = y[:, 128 * np : 128 * np + 128]
+            for n, x in enumerate(pair(x[:64], x[64:])):
+                sums.append(result[every8(2 * np + n, 64), :] + x)
+        for n, x in enumerate(sums):
+            result[every8(n, 64), :] = x
 
     def total(x):
         x = jnp.sum(x.reshape(-1, 8, 128), axis=0)
@@ -378,6 +420,7 @@
         return jnp.broadcast_to(x[None], (rows // 8, 8, 128)).reshape(rows, 128)
 
     copies = transpose_slots(0)
+    prepare_inner()
     transpose_inner(f0)
     copies = transpose_end(0, copies, z0, 1)
     forward_inner(z0, fw)
@@ -397,15 +440,15 @@
     ww0 = column(sums, 64)
     alpha0 = zz0 / ww0
     forward_end(3, copies, fs)
-    fs[...] = fw[...] - each(alpha0, 512) * fs[...]
-    spread(fs)
-    copies = transpose_slots(4)
+    s1 = fw[...] - each(alpha0, 512) * fs[...]
+    fs[...] = s1
     z1 = z0[...] - alpha0[None] * q[...]
-    s1 = fs[...]
     zz = total(z1 * z1) * 0.5
     ss = total(s1 * s1)
     sw = total(s1 * fw[...])
     going = reduce_start(1, 0, jnp.where(lane8 < 32, zz, jnp.where(lane8 < 64, ss, sw)))
+    spread(fs)
+    copies = transpose_slots(4)
     transpose_inner(fs)
     going = reduce_start(1, 1, reduce_end(1, 0, going))
     transpose_end(4, copies, t, None)
@@ -425,14 +468,19 @@
 
     low = low_half((128, 128))
     for np in range(4):
+        at = slice(128 * np, 128 * np + 128)
         for source, out in ((z0, adjoint), (t, normal)):
-            x = jnp.where(low, source[:, 2 * np, :], source[:, 2 * np + 1, :]).T
+            out[at] = jnp.where(low, source[:, 2 * np, :], source[:, 2 * np + 1, :])
+        top, bottom = pair(f0[every8(2 * np, 64), :], f0[every8(2 * np + 1, 64), :])
+        residual[at] = jnp.concatenate([top, bottom], axis=0)
+
+
+def turn(*refs):
+    for source, out in zip(refs[:3], refs[3:]):
+        for np in range(4):
+            x = source[128 * np : 128 * np + 128].T
             out[every8(2 * np, 64), :] = x[:64]
             out[every8(2 * np + 1, 64), :] = x[64:]
-        top, bottom = pair(f0[every8(2 * np, 64), :], f0[every8(2 * np + 1, 64), :])
-        x = jnp.concatenate([top, bottom], axis=0).T
-        residual[every8(2 * np, 64), :] = x[:64]
-        residual[every8(2 * np + 1, 64), :] = x[64:]
 
 
 def shards(
@@ -453,10 +501,6 @@
     paired_rows = jnp.sum(
         jnp.where(contact_pair[0][:, None] == slot[None, :], contact_rows[:, None], 0), axis=0
     )
-    sends = jnp.concatenate([send_blocks, contact_send])[None]
-    rows = jnp.concatenate(
-        [face_rows[:32], paired_rows[:32], face_rows[32:], paired_rows[32:]]
-    )[None]
     smem = pl.BlockSpec(memory_space=pltpu.SMEM)
     vmem = pl.BlockSpec(memory_space=pltpu.VMEM)
     copies = sum(size - 1 for size in stage_sizes(devices))
@@ -464,20 +508,24 @@
     outs = pl.pallas_call(
         functools.partial(kernel, devices),
         out_shape=[out] * 3,
-        in_specs=[smem] * 4 + [vmem] * 8,
+        in_specs=[smem] * 4 + [vmem] * 7 + [pl.BlockSpec(memory_space=pl.ANY)] * 3,
         out_specs=[vmem] * 3,
         scratch_shapes=[
+            pltpu.VMEM(inner_tiles.shape, BF16),
+            pltpu.VMEM(face_tiles.shape, BF16),
+            pltpu.VMEM(contact_tiles.shape, BF16),
             pltpu.VMEM((8192, 128), F32),
             pltpu.VMEM((8192, 128), F32),
             pltpu.VMEM((8192, 256), BF16),
             pltpu.VMEM((4096, 128), F32),
             pltpu.VMEM((4096, 128), BF16),
-            pltpu.VMEM((128, 512), BF16),
-            pltpu.VMEM((128, 128), BF16),
-            pltpu.VMEM((128, 128), BF16),
-            pltpu.VMEM((128, 128), BF16),
+            pltpu.VMEM((128, 1024), BF16),
+            pltpu.VMEM((128, 256), BF16),
+            pltpu.VMEM((128, 256), BF16),
+            pltpu.VMEM((128, 256), BF16),
             pltpu.VMEM((1024, 128), F32),
             pltpu.VMEM((1024, 128), F32),
+            pltpu.VMEM((128, 512), F32),
             pltpu.VMEM((128, 8, 128), F32),
             pltpu.VMEM((128, 8, 128), F32),
             pltpu.VMEM((128, 8, 128), F32),
@@ -496,6 +544,7 @@
             pltpu.SemaphoreType.DMA((APPS, 3)),
             pltpu.SemaphoreType.DMA((2, copies)),
             pltpu.SemaphoreType.DMA((2, copies)),
+            pltpu.SemaphoreType.DMA((3,)),
         ],
         compiler_params=pltpu.CompilerParams(
             collective_id=0, has_side_effects=True, vmem_limit_bytes=56 * 1024 * 1024
@@ -506,14 +555,19 @@
         paired_rows,
         face_counts,
         rhs.reshape(512, 128),
+        inner_cols,
+        send_blocks[None],
+        contact_send[None],
+        face_rows[None],
+        paired_rows[None],
+        contact_pair,
         inner_tiles,
-        inner_cols,
-        sends,
-        rows,
-        contact_pair,
         face_tiles,
         contact_tiles,
     )
+    outs = pl.pallas_call(
+        turn, out_shape=[out] * 3, in_specs=[vmem] * 3, out_specs=[vmem] * 3
+    )(*outs)
     return tuple(x.reshape(64, 8, 128) for x in outs)
 
 

time: 89 us -> 64 us (0.72)
  Pallas kernels: 79.3 us -> 61.8 us
  local copies, waits for them, and re-layouts: 5.81 us -> 0 us
  other arithmetic: 2.62 us -> 1.28 us
    pallas_call x1, Pallas kernels: 79.3 us -> 59.7 us  [shards(): pl.pallas_call(functools.partial(kernel, devices), out_shape=[out] * 3, i...]
    unnamed x5 -> x0, local copies, waits for them, and re-layouts: 5.01 us -> none
    pallas_call x0 -> x1, Pallas kernels: none -> 2.12 us  [shards(): pl.pallas_call(turn, out_shape=[out] * 3, in_specs=[vmem] * 3, out_specs=...]
    broadcast_in_dim x2 -> x0, other arithmetic: 1.85 us -> none  [the longest x1 1.26 us: shards(): sends = jnp.concatenate([send_blocks, contact_send])[None]]
where the time goes in v2:
time: 64 us; the launch traced here: 63.7 us
  Pallas kernels  61.8 us (97%)
  other arithmetic  1.28 us (2%)
  between operations  0.64 us (1%)
    pallas_call x1, Pallas kernels, shards(): pl.pallas_call(functools.partial(kernel, devices), out_shape=[out] * 3, i...  59.7 us
    pallas_call x1, Pallas kernels, shards(): pl.pallas_call(turn, out_shape=[out] * 3, in_specs=[vmem] * 3, out_specs=...  2.12 us
    reduce_sum x1, other arithmetic, shards(): jnp.sum(jnp.where(contact_pair[0][:, None] == slot[None, :], contact_rows...  1.28 us

profile of v2, /device:TPU:1, one launch (start us, length us, event | category | flops | bytes accessed | tf_op | source)
XLA Modules:
  0.0 63.7 jit_solution(14967523473392099310)
XLA Ops:
  0.6 1.3 %select_reduce_fusion.crows_s = s32[64]{0:T(128)} fusion(s32[64]{0:T(128)} %param.19, s32[64]{0:T(128)} %bitcast.12), kind=kLoop, calls=%fused_computation | loop fusion | flops 12224 | bytes 768 | tf_op jit(solution)/shard_map/reduce_sum | solution.py:501
  1.9 59.7 %shard_map.130 = (f32[512,128]{1,0:T(8,128)}, f32[512,128]{1,0:T(8,128)}, f32[512,128]{1,0:T(8,128)}) custom-call(s32[4,128]{1,0:T(4,128)} %cols_v.1, s32[64]{0:T(128)} %frows_s.1, s32[64]{0:T(128)} %select_reduce_fusion.crows_s, s32[1,2]{1,0:T(1,128)} %counts_s.1, f32[512,128]{1,0:T(8,128)} %bitcast.9, s32[4,128]{1,0:T(4,128)} %cols_v.1, s32[1,64]{1,0:T(1,128)} %bitcast.13, ...), custom_call_target="tpu_custom_call" | custom-call | tf_op jit(solution)/shard_map/pallas_call | solution.py:508
  61.6 2.1 %shard_map.131 = (f32[512,128]{1,0:T(8,128)}, f32[512,128]{1,0:T(8,128)}, f32[512,128]{1,0:T(8,128)}) custom-call(f32[512,128]{1,0:T(8,128)} %get-tuple-element.9.refs_0_, f32[512,128]{1,0:T(8,128)} %get-tuple-element.10.refs_1_, f32[512,128]{1,0:T(8,128)} %get-tuple-element.11.refs_2_), custom_call_target="tpu_custom_call" | custom-call | tf_op jit(solution)/shard_map/pallas_call | solution.py:568

commit v3 on v2

--- a/solution.py
+++ b/solution.py
@@ -11,6 +11,7 @@
 BF16 = jnp.bfloat16
 APPS = 5
 MESH = pl.DeviceIdType.MESH
+PAD = 136
 NT = (((1,), (1,)), ((), ()))
 
 
@@ -106,7 +107,6 @@
     zs,
     z0,
     q,
-    t,
     f0,
     fw,
     fs,
@@ -151,6 +151,7 @@
         return [me + (lax.rem(mine + i, size) - mine) * stride for i in range(1, size)]
 
     peers = [group_peers(stage) for stage in range(3)]
+    ar_first = [sum(size - 1 for size in sizes[:stage]) for stage in range(3)]
     everyone = [lower, upper, partner] + peers[0] + peers[1] + peers[2]
 
     barrier = pltpu.get_barrier_semaphore()
@@ -158,7 +159,6 @@
         pl.semaphore_signal(barrier, inc=1, device_id=place(other), device_id_type=MESH)
 
     row_id = lax.broadcasted_iota(jnp.int32, (128, 128), 0)
-    lane_id = lax.broadcasted_iota(jnp.int32, (128, 128), 1)
     for half in range(2):
         for k in range(4):
             at = half * 512 + k * 128
@@ -171,23 +171,20 @@
     picks = jnp.concatenate([frows_v[...], crows_v[...]], axis=1) == row_id
     picks = jnp.where(picks, 1.0, 0.0).astype(BF16)
     ohr[...] = jnp.concatenate([picks] * 2, axis=1)
-    eye = jnp.where(row_id == lane_id, 1.0, 0.0).astype(BF16)
 
     def prepare(a, carry):
         for half, out in ((0, wf0), (1, wf1)):
             x = tiles[2 * half : 2 * half + 2, a].reshape(128, 128)
-            x = turned(half, x)
-            out[pl.ds(a, 64, stride=128), :] = x[:64]
-            out[pl.ds(64 + a, 64, stride=128), :] = x[64:]
+            x = x.astype(F32).T
+            out[pl.ds(a, 64, stride=PAD), :] = x[:64]
+            out[pl.ds(64 + a, 64, stride=PAD), :] = x[64:]
         return carry
-
-    def turned(half, x):
-        return x.astype(F32).T if half else dot_nt(eye, x)
 
     def pack(i, carry):
         at = pl.ds(pl.multiple_of(i * 128, 128), 128)
-        w[at, 0:128] = wf0[at, :].astype(BF16)
-        w[at, 128:256] = wf1[at, :].astype(BF16)
+        padded = pl.ds(pl.multiple_of(i * PAD, 8), 128)
+        w[at, 0:128] = wf0[padded, :].astype(BF16)
+        w[at, 128:256] = wf1[padded, :].astype(BF16)
         return carry
 
     def prepare_inner():
@@ -207,19 +204,21 @@
     side_b = (slot >= 32) & (slot - 32 < counts_s[0, 1])
     face_pick = jnp.where((slot == other_slot) & (side_a | side_b), 1.0, 0.0)
     contact_pick = jnp.where(pair_v[...] == slot, 1.0, 0.0)
-    slot_pick = jnp.concatenate([face_pick, contact_pick], axis=0).astype(BF16)
+    slot_picks = (face_pick.astype(BF16), contact_pick.astype(BF16))
 
     def prepare_slots(i, carry):
-        parts = []
-        for n in range(4):
-            parts += [ftiles[4 * i + n], ctiles[4 * i + n]]
-        x = dot_nt(slot_pick, jnp.concatenate(parts, axis=0))
-        for n in range(4):
-            a = 4 * i + n
-            y = x[:, 128 * n : 128 * n + 128]
-            y = jnp.where(low_half((64, 128)), y[:64], y[64:])
-            ef[pl.ds(a, 32, stride=128), :] = y[:32]
-            ef[pl.ds(64 + a, 32, stride=128), :] = y[32:]
+        for kind, source in enumerate((ftiles, ctiles)):
+            parts = []
+            for n in range(4):
+                parts += [source[4 * i + n]] * 2
+            x = dot_nt(slot_picks[kind], jnp.concatenate(parts, axis=0))
+            for n in range(4):
+                y = x[:, 128 * n : 128 * n + 128]
+                for s2 in range(2):
+                    at = 32 * s2
+                    ef[pl.ds(kind * 16 * PAD + s2 * 64 + 4 * i + n, 16, stride=PAD), :] = jnp.where(
+                        low_half((16, 128)), y[at : at + 16], y[at + 16 : at + 32]
+                    )
         return carry
 
     for fetch in fetches[:2]:
@@ -228,7 +227,7 @@
 
     def pack_slots(i, carry):
         at = pl.ds(pl.multiple_of(i * 128, 128), 128)
-        e[at, :] = ef[at, :].astype(BF16)
+        e[at, :] = ef[pl.ds(pl.multiple_of(i * PAD, 8), 128), :].astype(BF16)
         return carry
 
     lax.fori_loop(0, 32, pack_slots, 0, unroll=4)
@@ -246,13 +245,13 @@
         u[0:64] = jnp.where(low, x, y).reshape(64, 8, 128)
         u[64:128] = jnp.where(low, y, x).reshape(64, 8, 128)
 
-    pl.semaphore_wait(barrier, len(everyone))
-
-    def exchange(app):
+
+    routes = ((lower, 0, 32, 32), (upper, 32, 64, 0), (partner, 64, 128, 64))
+
+    def exchange(app, kind):
         copies = []
-        for index, (other, start, stop, to) in enumerate(
-            ((lower, 0, 32, 32), (upper, 32, 64, 0), (partner, 64, 128, 64))
-        ):
+        for index in ((0, 1), (2,))[kind]:
+            other, start, stop, to = routes[index]
             copy = pltpu.make_async_remote_copy(
                 src_ref=sbuf.at[app, :, pl.ds(start, stop - start), :],
                 dst_ref=rbuf.at[app, :, pl.ds(to, stop - start), :],
@@ -265,51 +264,54 @@
             copies.append(copy)
         return copies
 
-    def reduce_start(which, stage, value):
+    def reduce_start(which, step, value):
+        stage = (1, 0, 2)[step]
         arsend[which, stage] = value
-        first = sum(size - 1 for size in sizes[:stage])
-        copies = []
         for index, other in enumerate(peers[stage]):
-            copy = pltpu.make_async_remote_copy(
+            pltpu.make_async_remote_copy(
                 src_ref=arsend.at[which, stage],
-                dst_ref=arrecv.at[which, first + index],
-                send_sem=asend.at[which, first + index],
-                recv_sem=arecv.at[which, first + index],
+                dst_ref=arrecv.at[which, ar_first[stage] + index],
+                send_sem=asend.at[which, stage],
+                recv_sem=arecv.at[which, stage],
                 device_id=place(other),
                 device_id_type=MESH,
-            )
-            copy.start()
-            copies.append(copy)
+            ).start()
+
+    def reduce_end(which, step):
+        stage = (1, 0, 2)[step]
+        arrived = arrecv.at[which, pl.ds(ar_first[stage], len(peers[stage]))]
+        pltpu.make_async_copy(arrived, arrived, arecv.at[which, stage]).wait()
+        pltpu.make_async_copy(arrived, arrived, asend.at[which, stage]).wait()
+        total = arsend[which, stage]
+        for index in range(len(peers[stage])):
+            total = total + arrecv[which, ar_first[stage] + index]
+        return total
+
+    def transpose_slots(app):
+        copies = []
+        for kind, rows in enumerate((frows_s, crows_s)):
+
+            def body(tp, carry):
+                parts = []
+                for h in range(2):
+                    parts.append(jnp.where(low8, u[rows[16 * h + tp]], zero8))
+                    parts.append(jnp.where(low8, zero8, u[rows[32 + 16 * h + tp]]))
+                out = split_dot(dot, jnp.concatenate(parts, axis=0), tile_at(e, 16 * kind + tp))
+                put8(ps, 32 * kind + tp, jnp.where(low8, out[0:8], out[16:24]))
+                put8(ps, 32 * kind + 16 + tp, jnp.where(low8, out[8:16], out[24:32]))
+                return carry
+
+            lax.fori_loop(0, 16, body, 0, unroll=16)
+            for np in range(4):
+                at = 256 * kind + 2 * np
+                x, y = pair(ps[every8(at, 32), :], ps[every8(at + 1, 32), :])
+                sbuf[app, np, 64 * kind : 64 * kind + 64] = jnp.concatenate(
+                    [x[:16], y[:16], x[16:], y[16:]], axis=0
+                )
+            if app == 0 and kind == 0:
+                pl.semaphore_wait(barrier, len(everyone))
+            copies += exchange(app, kind)
         return copies
-
-    def reduce_end(which, stage, copies):
-        for copy in copies:
-            copy.wait()
-        total = arsend[which, stage]
-        first = sum(size - 1 for size in sizes[:stage])
-        for index in range(len(copies)):
-            total = total + arrecv[which, first + index]
-        return total
-
-    def transpose_slots(app):
-        def body(sp, carry):
-            parts = [
-                jnp.where(low8, u[frows_s[sp]], zero8),
-                jnp.where(low8, zero8, u[frows_s[32 + sp]]),
-                jnp.where(low8, u[crows_s[sp]], zero8),
-                jnp.where(low8, zero8, u[crows_s[32 + sp]]),
-            ]
-            out = split_dot(dot, jnp.concatenate(parts, axis=0), tile_at(e, sp))
-            put8(ps, sp, jnp.where(low8, out[0:8], out[16:24]))
-            put8(ps, 32 + sp, jnp.where(low8, out[8:16], out[24:32]))
-            return carry
-
-        lax.fori_loop(0, 32, body, 0, unroll=8)
-        for np in range(4):
-            face, contact = pair(ps[every8(2 * np, 64), :], ps[every8(2 * np + 1, 64), :])
-            sbuf[app, np, 0:64] = face
-            sbuf[app, np, 64:128] = contact
-        return exchange(app)
 
     def transpose_inner(field):
         def body(jp, carry):
@@ -350,12 +352,15 @@
             x = dot(ohst[...], jnp.concatenate(split(z), axis=0))
             for np in range(4):
                 sbuf[send_app, np] = x[:, 128 * np : 128 * np + 128]
-            copies = exchange(send_app)
+            copies = exchange(send_app, 0) + exchange(send_app, 1)
         for np in range(4):
             x = z[:, 128 * np : 128 * np + 128]
-            other = swap(x)
-            result[:, 2 * np, :] = jnp.where(low, x, other)
-            result[:, 2 * np + 1, :] = jnp.where(low, other, x)
+            if result is None:
+                p01[128 * np : 128 * np + 128] = x
+            else:
+                other = swap(x)
+                result[:, 2 * np, :] = jnp.where(low, x, other)
+                result[:, 2 * np + 1, :] = jnp.where(low, other, x)
         return copies
 
     def forward_inner(field, result):
@@ -375,25 +380,31 @@
         lax.fori_loop(0, 64, body, 0, unroll=8)
 
     def forward_end(app, copies, result):
-        for copy in copies:
-            copy.wait()
         low = low_half((64, 128))
-        for np in range(4):
-            x = rbuf[app, np]
-            face, contact = x[:64], x[64:]
-            xf[every8(2 * np, 64), :] = jnp.where(low, face, 0.0)
-            xf[every8(2 * np + 1, 64), :] = jnp.where(low, swap(face), 0.0)
-            xf[every8(512 + 2 * np, 64), :] = jnp.where(low, 0.0, swap(contact))
-            xf[every8(512 + 2 * np + 1, 64), :] = jnp.where(low, 0.0, contact)
-
-        def body(sp, carry):
-            parts = [block8(xf, sp + 32 * i) for i in range(4)]
-            out = split_dot(dot_nt, jnp.concatenate(parts, axis=0), tile_at(e, sp))
-            put8(uo, sp, jnp.where(low8, out[0:8], out[8:16]))
-            put8(uo, 32 + sp, jnp.where(low8, out[16:24], out[24:32]))
-            return carry
-
-        lax.fori_loop(0, 32, body, 0, unroll=8)
+        first = lax.rem(lax.broadcasted_iota(jnp.int32, (64, 128), 0) // 16, 2) == 0
+        mine = low == first
+        for kind in (1, 0):
+            for copy in (copies[:2], copies[2:])[kind]:
+                copy.wait()
+            for np in range(4):
+                x = rbuf[app, np, 64 * kind : 64 * kind + 64]
+                y = swap(x)
+                at = 512 * kind + 2 * np
+                xf[every8(at, 64), :] = jnp.where(mine, jnp.where(first, x, y), 0.0)
+                xf[every8(at + 1, 64), :] = jnp.where(mine, jnp.where(first, y, x), 0.0)
+
+            def body(tp, carry):
+                parts = []
+                for h in range(2):
+                    for s2 in range(2):
+                        parts.append(block8(xf, 64 * kind + 32 * s2 + 16 * h + tp))
+                tile = tile_at(e, 16 * kind + tp)
+                out = split_dot(dot_nt, jnp.concatenate(parts, axis=0), tile)
+                put8(uo, 32 * kind + tp, jnp.where(low8, out[0:8], out[8:16]))
+                put8(uo, 32 * kind + 16 + tp, jnp.where(low8, out[16:24], out[24:32]))
+                return carry
+
+            lax.fori_loop(0, 16, body, 0, unroll=16)
         parts = []
         for np in range(4):
             s0, s1 = pair(uo[every8(2 * np, 64), :], uo[every8(2 * np + 1, 64), :])
@@ -427,52 +438,68 @@
     zz = total(z0[...] * z0[...]) * 0.5
     forward_end(1, copies, fw)
     ww = total(fw[...] * fw[...])
-    going = reduce_start(0, 0, jnp.where(lane8 < 64, zz, ww))
+    reduce_start(0, 0, jnp.where(lane8 < 64, zz, ww))
     spread(fw)
     copies = transpose_slots(2)
-    going = reduce_start(0, 1, reduce_end(0, 0, going))
     transpose_inner(fw)
-    going = reduce_start(0, 2, reduce_end(0, 1, going))
+    reduce_start(0, 1, reduce_end(0, 0))
     copies = transpose_end(2, copies, q, 3)
     forward_inner(q, fs)
-    sums = reduce_end(0, 2, going)
+    reduce_start(0, 2, reduce_end(0, 1))
+    forward_end(3, copies, fs)
+    sums = reduce_end(0, 2)
     zz0 = column(sums, 0)
     ww0 = column(sums, 64)
     alpha0 = zz0 / ww0
-    forward_end(3, copies, fs)
     s1 = fw[...] - each(alpha0, 512) * fs[...]
     fs[...] = s1
     z1 = z0[...] - alpha0[None] * q[...]
     zz = total(z1 * z1) * 0.5
     ss = total(s1 * s1)
     sw = total(s1 * fw[...])
-    going = reduce_start(1, 0, jnp.where(lane8 < 32, zz, jnp.where(lane8 < 64, ss, sw)))
+    reduce_start(1, 0, jnp.where(lane8 < 32, zz, jnp.where(lane8 < 64, ss, sw)))
     spread(fs)
     copies = transpose_slots(4)
     transpose_inner(fs)
-    going = reduce_start(1, 1, reduce_end(1, 0, going))
-    transpose_end(4, copies, t, None)
-    going = reduce_start(1, 2, reduce_end(1, 1, going))
-    sums = reduce_end(1, 2, going)
+    reduce_start(1, 1, reduce_end(1, 0))
+    transpose_end(4, copies, None, None)
+    reduce_start(1, 2, reduce_end(1, 1))
+
+    def by_lanes(x, np):
+        return jnp.where(lane8[:1] < 64, x[2 * np : 2 * np + 1], x[2 * np + 1 : 2 * np + 2])
+
+    def gather_rows(field, np):
+        top, bottom = pair(field[every8(2 * np, 64), :], field[every8(2 * np + 1, 64), :])
+        return jnp.concatenate([top, bottom], axis=0)
+
+    low = low_half((128, 128))
+    for np in range(4):
+        at = slice(128 * np, 128 * np + 128)
+        more = slice(512 + 128 * np, 512 + 128 * np + 128)
+        a0 = by_lanes(alpha0, np)
+        x = jnp.where(low, z0[:, 2 * np, :], z0[:, 2 * np + 1, :])
+        y = jnp.where(low, q[:, 2 * np, :], q[:, 2 * np + 1, :])
+        adjoint[at] = x
+        normal[at] = x - a0 * y
+        p01[more] = y
+        x = gather_rows(fw, np)
+        residual[at] = gather_rows(f0, np) - a0 * x
+        p23[at] = x
+        p23[more] = gather_rows(fs, np)
+
+    sums = reduce_end(1, 2)
     zz1 = column(sums, 0)
     beta = zz1 / zz0
     ww1 = column(sums, 32) + beta * (2.0 * column(sums, 64) + beta * ww0)
     alpha1 = zz1 / ww1
-
-    a0, a1, b = (x[None] for x in (alpha0, alpha1, beta))
-    z1 = z0[...] - a0 * q[...]
-    t[...] = z1 - a1 * (t[...] + b * q[...])
-    z0[...] = a0 * z0[...] + a1 * (z1 + b * z0[...])
-    a0, a1, b = (each(x, 512) for x in (alpha0, alpha1, beta))
-    f0[...] = f0[...] - a0 * fw[...] - a1 * (fs[...] + b * fw[...])
-
-    low = low_half((128, 128))
     for np in range(4):
         at = slice(128 * np, 128 * np + 128)
-        for source, out in ((z0, adjoint), (t, normal)):
-            out[at] = jnp.where(low, source[:, 2 * np, :], source[:, 2 * np + 1, :])
-        top, bottom = pair(f0[every8(2 * np, 64), :], f0[every8(2 * np + 1, 64), :])
-        residual[at] = jnp.concatenate([top, bottom], axis=0)
+        more = slice(512 + 128 * np, 512 + 128 * np + 128)
+        a0, a1, b = (by_lanes(x, np) for x in (alpha0, alpha1, beta))
+        x, z1 = adjoint[at], normal[at]
+        adjoint[at] = a0 * x + a1 * (z1 + b * x)
+        normal[at] = z1 - a1 * (p01[at] + b * p01[more])
+        residual[at] = residual[at] - a1 * (p23[more] + b * p23[at])
 
 
 def turn(*refs):
@@ -514,10 +541,10 @@
             pltpu.VMEM(inner_tiles.shape, BF16),
             pltpu.VMEM(face_tiles.shape, BF16),
             pltpu.VMEM(contact_tiles.shape, BF16),
-            pltpu.VMEM((8192, 128), F32),
-            pltpu.VMEM((8192, 128), F32),
+            pltpu.VMEM((64 * PAD, 128), F32),
+            pltpu.VMEM((64 * PAD, 128), F32),
             pltpu.VMEM((8192, 256), BF16),
-            pltpu.VMEM((4096, 128), F32),
+            pltpu.VMEM((32 * PAD, 128), F32),
             pltpu.VMEM((4096, 128), BF16),
             pltpu.VMEM((128, 1024), BF16),
             pltpu.VMEM((128, 256), BF16),
@@ -526,7 +553,6 @@
             pltpu.VMEM((1024, 128), F32),
             pltpu.VMEM((1024, 128), F32),
             pltpu.VMEM((128, 512), F32),
-            pltpu.VMEM((128, 8, 128), F32),
             pltpu.VMEM((128, 8, 128), F32),
             pltpu.VMEM((128, 8, 128), F32),
             pltpu.VMEM((512, 128), F32),
@@ -542,8 +568,8 @@
             pltpu.VMEM((2, copies, 8, 128), F32),
             pltpu.SemaphoreType.DMA((APPS, 3)),
             pltpu.SemaphoreType.DMA((APPS, 3)),
-            pltpu.SemaphoreType.DMA((2, copies)),
-            pltpu.SemaphoreType.DMA((2, copies)),
+            pltpu.SemaphoreType.DMA((2, 3)),
+            pltpu.SemaphoreType.DMA((2, 3)),
             pltpu.SemaphoreType.DMA((3,)),
         ],
         compiler_params=pltpu.CompilerParams(

time: 64 us -> 56.3 us (0.88)
  Pallas kernels: 61.8 us -> 54.2 us
    pallas_call x1, Pallas kernels: 59.7 us -> 52.1 us  [shards(): pl.pallas_call(functools.partial(kernel, devices), out_shape=[out] * 3, i...]
where the time goes in v3:
time: 56.3 us; the launch traced here: 56.2 us
  Pallas kernels  54.2 us (96%)
  other arithmetic  1.28 us (2%)
  between operations  0.64 us (1%)
    pallas_call x1, Pallas kernels, shards(): pl.pallas_call(functools.partial(kernel, devices), out_shape=[out] * 3, i...  52.1 us
    pallas_call x1, Pallas kernels, shards(): pl.pallas_call(turn, out_shape=[out] * 3, in_specs=[vmem] * 3, out_specs=...  2.12 us
    reduce_sum x1, other arithmetic, shards(): jnp.sum(jnp.where(contact_pair[0][:, None] == slot[None, :], contact_rows...  1.28 us

profile of v3, /device:TPU:1, one launch (start us, length us, event | category | flops | bytes accessed | tf_op | source)
XLA Modules:
  0.0 56.2 jit_solution(7898822555801352307)
XLA Ops:
  0.6 1.3 %select_reduce_fusion.crows_s = s32[64]{0:T(128)} fusion(s32[64]{0:T(128)} %param.19, s32[64]{0:T(128)} %bitcast.12), kind=kLoop, calls=%fused_computation | loop fusion | flops 12224 | bytes 768 | tf_op jit(solution)/shard_map/reduce_sum | solution.py:528
  1.9 52.1 %shard_map.130 = (f32[512,128]{1,0:T(8,128)}, f32[512,128]{1,0:T(8,128)}, f32[512,128]{1,0:T(8,128)}) custom-call(s32[4,128]{1,0:T(4,128)} %cols_v.1, s32[64]{0:T(128)} %frows_s.1, s32[64]{0:T(128)} %select_reduce_fusion.crows_s, s32[1,2]{1,0:T(1,128)} %counts_s.1, f32[512,128]{1,0:T(8,128)} %bitcast.9, s32[4,128]{1,0:T(4,128)} %cols_v.1, s32[1,64]{1,0:T(1,128)} %bitcast.13, ...), custom_call_target="tpu_custom_call" | custom-call | tf_op jit(solution)/shard_map/pallas_call | solution.py:535
  54.0 2.1 %shard_map.131 = (f32[512,128]{1,0:T(8,128)}, f32[512,128]{1,0:T(8,128)}, f32[512,128]{1,0:T(8,128)}) custom-call(f32[512,128]{1,0:T(8,128)} %get-tuple-element.9.refs_0_, f32[512,128]{1,0:T(8,128)} %get-tuple-element.10.refs_1_, f32[512,128]{1,0:T(8,128)} %get-tuple-element.11.refs_2_), custom_call_target="tpu_custom_call" | custom-call | tf_op jit(solution)/shard_map/pallas_call | solution.py:594

commit v4 on v3

--- a/solution.py
+++ b/solution.py
@@ -75,7 +75,6 @@
     devices,
     cols_s,
     frows_s,
-    crows_s,
     counts_s,
     rhs,
     cols_v,
@@ -123,6 +122,9 @@
     asend,
     arecv,
     fetched,
+    crows_w,
+    crows_s,
+    crows_sem,
 ):
     fetches = [
         pltpu.make_async_copy(source, target, fetched.at[index])
@@ -159,18 +161,30 @@
         pl.semaphore_signal(barrier, inc=1, device_id=place(other), device_id_type=MESH)
 
     row_id = lax.broadcasted_iota(jnp.int32, (128, 128), 0)
-    for half in range(2):
-        for k in range(4):
-            at = half * 512 + k * 128
-            ohk[:, at : at + 128] = jnp.where(cols_v[k : k + 1, :] == row_id, 1.0, 0.0).astype(BF16)
-    picks = jnp.concatenate([send_v[...], csend_v[...]], axis=1) == row_id
-    picks = jnp.where(picks, 1.0, 0.0)
-    ohs[...] = jnp.concatenate([picks.astype(BF16)] * 2, axis=1)
-    picks = picks.T.astype(BF16)
-    ohst[...] = jnp.concatenate([picks] * 2, axis=1)
-    picks = jnp.concatenate([frows_v[...], crows_v[...]], axis=1) == row_id
-    picks = jnp.where(picks, 1.0, 0.0).astype(BF16)
-    ohr[...] = jnp.concatenate([picks] * 2, axis=1)
+
+    def order_contacts():
+        lane_id = lax.broadcasted_iota(jnp.int32, (128, 128), 1)
+        matches = jnp.broadcast_to(jnp.concatenate([pair_v[...]] * 2, axis=1), (128, 128)).T == lane_id
+        rows = jnp.broadcast_to(jnp.concatenate([crows_v[...]] * 2, axis=1), (128, 128)).T
+        rows = jnp.sum(jnp.where(matches & (row_id < 64), rows, 0), axis=0, keepdims=True)
+        crows_w[...] = jnp.broadcast_to(rows, (8, 128))
+        hand = pltpu.make_async_copy(crows_w, crows_s, crows_sem)
+        hand.start()
+        hand.wait()
+
+    def prepare_picks():
+        for half in range(2):
+            for k in range(4):
+                at = half * 512 + k * 128
+                ohk[:, at : at + 128] = jnp.where(cols_v[k : k + 1, :] == row_id, 1.0, 0.0).astype(BF16)
+        picks = jnp.concatenate([send_v[...], csend_v[...]], axis=1) == row_id
+        picks = jnp.where(picks, 1.0, 0.0)
+        ohs[...] = jnp.concatenate([picks.astype(BF16)] * 2, axis=1)
+        picks = picks.T.astype(BF16)
+        ohst[...] = jnp.concatenate([picks] * 2, axis=1)
+        picks = jnp.concatenate([frows_v[...], crows_w[0:1, :64]], axis=1) == row_id
+        picks = jnp.where(picks, 1.0, 0.0).astype(BF16)
+        ohr[...] = jnp.concatenate([picks] * 2, axis=1)
 
     def prepare(a, carry):
         for half, out in ((0, wf0), (1, wf1)):
@@ -206,8 +220,10 @@
     contact_pick = jnp.where(pair_v[...] == slot, 1.0, 0.0)
     slot_picks = (face_pick.astype(BF16), contact_pick.astype(BF16))
 
-    def prepare_slots(i, carry):
-        for kind, source in enumerate((ftiles, ctiles)):
+    def prepare_slots(kind):
+        source = (ftiles, ctiles)[kind]
+
+        def turn_four(i, carry):
             parts = []
             for n in range(4):
                 parts += [source[4 * i + n]] * 2
@@ -219,18 +235,16 @@
                     ef[pl.ds(kind * 16 * PAD + s2 * 64 + 4 * i + n, 16, stride=PAD), :] = jnp.where(
                         low_half((16, 128)), y[at : at + 16], y[at + 16 : at + 32]
                     )
-        return carry
-
-    for fetch in fetches[:2]:
-        fetch.wait()
-    lax.fori_loop(0, 16, prepare_slots, 0, unroll=2)
-
-    def pack_slots(i, carry):
-        at = pl.ds(pl.multiple_of(i * 128, 128), 128)
-        e[at, :] = ef[pl.ds(pl.multiple_of(i * PAD, 8), 128), :].astype(BF16)
-        return carry
-
-    lax.fori_loop(0, 32, pack_slots, 0, unroll=4)
+            return carry
+
+        def pack_slots(i, carry):
+            at = pl.ds(pl.multiple_of(i * 128, 128), 128)
+            e[at, :] = ef[pl.ds(pl.multiple_of(i * PAD, 8), 128), :].astype(BF16)
+            return carry
+
+        fetches[kind].wait()
+        lax.fori_loop(0, 16, turn_four, 0, unroll=4)
+        lax.fori_loop(16 * kind, 16 * kind + 16, pack_slots, 0, unroll=4)
 
     def tile_at(ref, index):
         return ref[pl.ds(pl.multiple_of(index * 128, 128), 128), :]
@@ -289,13 +303,15 @@
 
     def transpose_slots(app):
         copies = []
-        for kind, rows in enumerate((frows_s, crows_s)):
+        if app == 0:
+            prepare_slots(0)
+        for kind, rows in enumerate((lambda i: frows_s[i], lambda i: crows_s[0, i])):
 
             def body(tp, carry):
                 parts = []
                 for h in range(2):
-                    parts.append(jnp.where(low8, u[rows[16 * h + tp]], zero8))
-                    parts.append(jnp.where(low8, zero8, u[rows[32 + 16 * h + tp]]))
+                    parts.append(jnp.where(low8, u[rows(16 * h + tp)], zero8))
+                    parts.append(jnp.where(low8, zero8, u[rows(32 + 16 * h + tp)]))
                 out = split_dot(dot, jnp.concatenate(parts, axis=0), tile_at(e, 16 * kind + tp))
                 put8(ps, 32 * kind + tp, jnp.where(low8, out[0:8], out[16:24]))
                 put8(ps, 32 * kind + 16 + tp, jnp.where(low8, out[8:16], out[24:32]))
@@ -311,6 +327,9 @@
             if app == 0 and kind == 0:
                 pl.semaphore_wait(barrier, len(everyone))
             copies += exchange(app, kind)
+            if app == 0 and kind == 0:
+                order_contacts()
+                prepare_slots(1)
         return copies
 
     def transpose_inner(field):
@@ -331,7 +350,12 @@
             put8(p23, 64 + jp, y[:, 128:])
             return carry
 
-        lax.fori_loop(0, 64, body, 0, unroll=8)
+        lax.fori_loop(0, 64, body, 0, unroll=16)
+
+    def put_turned(out, first, np, x):
+        x = x.T
+        out[every8(first + 2 * np, 64), :] = x[:64]
+        out[every8(first + 2 * np + 1, 64), :] = x[64:]
 
     def halves(parts):
         x = jnp.concatenate(parts, axis=1)
@@ -349,14 +373,18 @@
         low = low_half((128, 128))
         z = zs[...] + dot(ohs[...], halves([rbuf[app, np] for np in range(4)]))
         if send_app is not None:
-            x = dot(ohst[...], jnp.concatenate(split(z), axis=0))
-            for np in range(4):
-                sbuf[send_app, np] = x[:, 128 * np : 128 * np + 128]
-            copies = exchange(send_app, 0) + exchange(send_app, 1)
+            terms = jnp.concatenate(split(z), axis=0)
+            copies = []
+            for kind in range(2):
+                at = slice(64 * kind, 64 * kind + 64)
+                x = dot(ohst[at], terms)
+                for np in range(4):
+                    sbuf[send_app, np, at] = x[:, 128 * np : 128 * np + 128]
+                copies += exchange(send_app, kind)
         for np in range(4):
             x = z[:, 128 * np : 128 * np + 128]
             if result is None:
-                p01[128 * np : 128 * np + 128] = x
+                put_turned(p01, 0, np, x)
             else:
                 other = swap(x)
                 result[:, 2 * np, :] = jnp.where(low, x, other)
@@ -377,7 +405,7 @@
             put8(result, jp, jnp.where(low8, out[0:8] + out[8:16], out[16:24] + out[24:32]))
             return carry
 
-        lax.fori_loop(0, 64, body, 0, unroll=8)
+        lax.fori_loop(0, 64, body, 0, unroll=16)
 
     def forward_end(app, copies, result):
         low = low_half((64, 128))
@@ -431,6 +459,7 @@
         return jnp.broadcast_to(x[None], (rows // 8, 8, 128)).reshape(rows, 128)
 
     copies = transpose_slots(0)
+    prepare_picks()
     prepare_inner()
     transpose_inner(f0)
     copies = transpose_end(0, copies, z0, 1)
@@ -465,49 +494,36 @@
     transpose_end(4, copies, None, None)
     reduce_start(1, 2, reduce_end(1, 1))
 
-    def by_lanes(x, np):
-        return jnp.where(lane8[:1] < 64, x[2 * np : 2 * np + 1], x[2 * np + 1 : 2 * np + 2])
-
     def gather_rows(field, np):
         top, bottom = pair(field[every8(2 * np, 64), :], field[every8(2 * np + 1, 64), :])
         return jnp.concatenate([top, bottom], axis=0)
 
     low = low_half((128, 128))
     for np in range(4):
-        at = slice(128 * np, 128 * np + 128)
-        more = slice(512 + 128 * np, 512 + 128 * np + 128)
-        a0 = by_lanes(alpha0, np)
-        x = jnp.where(low, z0[:, 2 * np, :], z0[:, 2 * np + 1, :])
-        y = jnp.where(low, q[:, 2 * np, :], q[:, 2 * np + 1, :])
-        adjoint[at] = x
-        normal[at] = x - a0 * y
-        p01[more] = y
-        x = gather_rows(fw, np)
-        residual[at] = gather_rows(f0, np) - a0 * x
-        p23[at] = x
-        p23[more] = gather_rows(fs, np)
+        for source, out, first in ((z0, adjoint, 0), (q, p01, 512)):
+            x = jnp.where(low, source[:, 2 * np, :], source[:, 2 * np + 1, :])
+            put_turned(out, first, np, x)
+        for source, out, first in ((f0, residual, 0), (fw, p23, 0), (fs, p23, 512)):
+            put_turned(out, first, np, gather_rows(source, np))
+    a0 = each(alpha0, 512)
+    normal[...] = adjoint[...] - a0 * p01[512:1024]
+    residual[...] = residual[...] - a0 * p23[0:512]
 
     sums = reduce_end(1, 2)
     zz1 = column(sums, 0)
     beta = zz1 / zz0
     ww1 = column(sums, 32) + beta * (2.0 * column(sums, 64) + beta * ww0)
     alpha1 = zz1 / ww1
-    for np in range(4):
-        at = slice(128 * np, 128 * np + 128)
-        more = slice(512 + 128 * np, 512 + 128 * np + 128)
-        a0, a1, b = (by_lanes(x, np) for x in (alpha0, alpha1, beta))
-        x, z1 = adjoint[at], normal[at]
-        adjoint[at] = a0 * x + a1 * (z1 + b * x)
-        normal[at] = z1 - a1 * (p01[at] + b * p01[more])
-        residual[at] = residual[at] - a1 * (p23[more] + b * p23[at])
-
-
-def turn(*refs):
+    a1, b = each(alpha1, 512), each(beta, 512)
+    x, z1 = adjoint[...], normal[...]
+    adjoint[...] = a0 * x + a1 * (z1 + b * x)
+    normal[...] = z1 - a1 * (p01[0:512] + b * p01[512:1024])
+    residual[...] = residual[...] - a1 * (p23[512:1024] + b * p23[0:512])
+
+
+def hand_over(*refs):
     for source, out in zip(refs[:3], refs[3:]):
-        for np in range(4):
-            x = source[128 * np : 128 * np + 128].T
-            out[every8(2 * np, 64), :] = x[:64]
-            out[every8(2 * np + 1, 64), :] = x[64:]
+        out[...] = source[...]
 
 
 def shards(
@@ -524,10 +540,6 @@
     contact_pair,
     contact_tiles,
 ):
-    slot = jnp.arange(64, dtype=jnp.int32)
-    paired_rows = jnp.sum(
-        jnp.where(contact_pair[0][:, None] == slot[None, :], contact_rows[:, None], 0), axis=0
-    )
     smem = pl.BlockSpec(memory_space=pltpu.SMEM)
     vmem = pl.BlockSpec(memory_space=pltpu.VMEM)
     copies = sum(size - 1 for size in stage_sizes(devices))
@@ -535,7 +547,7 @@
     outs = pl.pallas_call(
         functools.partial(kernel, devices),
         out_shape=[out] * 3,
-        in_specs=[smem] * 4 + [vmem] * 7 + [pl.BlockSpec(memory_space=pl.ANY)] * 3,
+        in_specs=[smem] * 3 + [vmem] * 7 + [pl.BlockSpec(memory_space=pl.ANY)] * 3,
         out_specs=[vmem] * 3,
         scratch_shapes=[
             pltpu.VMEM(inner_tiles.shape, BF16),
@@ -571,6 +583,9 @@
             pltpu.SemaphoreType.DMA((2, 3)),
             pltpu.SemaphoreType.DMA((2, 3)),
             pltpu.SemaphoreType.DMA((3,)),
+            pltpu.VMEM((8, 128), jnp.int32),
+            pltpu.SMEM((8, 128), jnp.int32),
+            pltpu.SemaphoreType.DMA,
         ],
         compiler_params=pltpu.CompilerParams(
             collective_id=0, has_side_effects=True, vmem_limit_bytes=56 * 1024 * 1024
@@ -578,21 +593,20 @@
     )(
         inner_cols,
         face_rows,
-        paired_rows,
         face_counts,
         rhs.reshape(512, 128),
         inner_cols,
         send_blocks[None],
         contact_send[None],
         face_rows[None],
-        paired_rows[None],
+        contact_rows[None],
         contact_pair,
         inner_tiles,
         face_tiles,
         contact_tiles,
     )
     outs = pl.pallas_call(
-        turn, out_shape=[out] * 3, in_specs=[vmem] * 3, out_specs=[vmem] * 3
+        hand_over, out_shape=[out] * 3, in_specs=[vmem] * 3, out_specs=[vmem] * 3
     )(*outs)
     return tuple(x.reshape(64, 8, 128) for x in outs)
 

time: 56.3 us -> 56.4 us (level)
  Pallas kernels: 54.2 us -> 55.6 us
  other arithmetic: 1.28 us -> 0 us
    pallas_call x1, Pallas kernels: 52.1 us -> 53.6 us  [shards(): pl.pallas_call(functools.partial(kernel, devices), out_shape=[out] * 3, i...]
    reduce_sum x1 -> x0, other arithmetic: 1.28 us -> none  [shards(): jnp.sum(jnp.where(contact_pair[0][:, None] == slot[None, :], contact_rows...]
where the time goes in v4:
time: 56.4 us; the launch traced here: 56.2 us
  Pallas kernels  55.6 us (99%)
  between operations  0.64 us (1%)
    pallas_call x1, Pallas kernels, shards(): pl.pallas_call(functools.partial(kernel, devices), out_shape=[out] * 3, i...  53.6 us
    pallas_call x1, Pallas kernels, shards(): pl.pallas_call(hand_over, out_shape=[out] * 3, in_specs=[vmem] * 3, out_s...  2 us

profile of v4, /device:TPU:1, one launch (start us, length us, event | category | flops | bytes accessed | tf_op | source)
XLA Modules:
  0.0 56.2 jit_solution(14727314362310661750)
XLA Ops:
  0.6 53.6 %shard_map.130 = (f32[512,128]{1,0:T(8,128)}, f32[512,128]{1,0:T(8,128)}, f32[512,128]{1,0:T(8,128)}) custom-call(s32[4,128]{1,0:T(4,128)} %cols_v.1, s32[64]{0:T(128)} %frows_s.1, s32[1,2]{1,0:T(1,128)} %counts_s.1, f32[512,128]{1,0:T(8,128)} %bitcast.8, s32[4,128]{1,0:T(4,128)} %cols_v.1, s32[1,64]{1,0:T(1,128)} %bitcast.10, s32[1,64]{1,0:T(1,128)} %bitcast.11, ...), custom_call_target="tpu_custom_call" | custom-call | tf_op jit(solution)/shard_map/pallas_call | solution.py:547
  54.2 2.0 %shard_map.131 = (f32[512,128]{1,0:T(8,128)}, f32[512,128]{1,0:T(8,128)}, f32[512,128]{1,0:T(8,128)}) custom-call(f32[512,128]{1,0:T(8,128)} %get-tuple-element.9.refs_0_, f32[512,128]{1,0:T(8,128)} %get-tuple-element.10.refs_1_, f32[512,128]{1,0:T(8,128)} %get-tuple-element.11.refs_2_), custom_call_target="tpu_custom_call" | custom-call | tf_op jit(solution)/shard_map/pallas_call | solution.py:608

commit v5 on v4

--- a/solution.py
+++ b/solution.py
@@ -161,30 +161,26 @@
         pl.semaphore_signal(barrier, inc=1, device_id=place(other), device_id_type=MESH)
 
     row_id = lax.broadcasted_iota(jnp.int32, (128, 128), 0)
-
-    def order_contacts():
-        lane_id = lax.broadcasted_iota(jnp.int32, (128, 128), 1)
-        matches = jnp.broadcast_to(jnp.concatenate([pair_v[...]] * 2, axis=1), (128, 128)).T == lane_id
-        rows = jnp.broadcast_to(jnp.concatenate([crows_v[...]] * 2, axis=1), (128, 128)).T
-        rows = jnp.sum(jnp.where(matches & (row_id < 64), rows, 0), axis=0, keepdims=True)
-        crows_w[...] = jnp.broadcast_to(rows, (8, 128))
-        hand = pltpu.make_async_copy(crows_w, crows_s, crows_sem)
-        hand.start()
-        hand.wait()
-
-    def prepare_picks():
-        for half in range(2):
-            for k in range(4):
-                at = half * 512 + k * 128
-                ohk[:, at : at + 128] = jnp.where(cols_v[k : k + 1, :] == row_id, 1.0, 0.0).astype(BF16)
-        picks = jnp.concatenate([send_v[...], csend_v[...]], axis=1) == row_id
-        picks = jnp.where(picks, 1.0, 0.0)
-        ohs[...] = jnp.concatenate([picks.astype(BF16)] * 2, axis=1)
-        picks = picks.T.astype(BF16)
-        ohst[...] = jnp.concatenate([picks] * 2, axis=1)
-        picks = jnp.concatenate([frows_v[...], crows_w[0:1, :64]], axis=1) == row_id
-        picks = jnp.where(picks, 1.0, 0.0).astype(BF16)
-        ohr[...] = jnp.concatenate([picks] * 2, axis=1)
+    for half in range(2):
+        for k in range(4):
+            at = half * 512 + k * 128
+            ohk[:, at : at + 128] = jnp.where(cols_v[k : k + 1, :] == row_id, 1.0, 0.0).astype(BF16)
+    picks = jnp.concatenate([send_v[...], csend_v[...]], axis=1) == row_id
+    picks = jnp.where(picks, 1.0, 0.0)
+    ohs[...] = jnp.concatenate([picks.astype(BF16)] * 2, axis=1)
+    picks = picks.T.astype(BF16)
+    ohst[...] = jnp.concatenate([picks] * 2, axis=1)
+    lane_id = lax.broadcasted_iota(jnp.int32, (128, 128), 1)
+    matches = jnp.broadcast_to(jnp.concatenate([pair_v[...]] * 2, axis=1), (128, 128)).T == lane_id
+    rows = jnp.broadcast_to(jnp.concatenate([crows_v[...]] * 2, axis=1), (128, 128)).T
+    rows = jnp.sum(jnp.where(matches & (row_id < 64), rows, 0), axis=0, keepdims=True)
+    crows_w[...] = jnp.broadcast_to(rows, (8, 128))
+    hand = pltpu.make_async_copy(crows_w, crows_s, crows_sem)
+    hand.start()
+    hand.wait()
+    picks = jnp.concatenate([frows_v[...], rows[:, :64]], axis=1) == row_id
+    picks = jnp.where(picks, 1.0, 0.0).astype(BF16)
+    ohr[...] = jnp.concatenate([picks] * 2, axis=1)
 
     def prepare(a, carry):
         for half, out in ((0, wf0), (1, wf1)):
@@ -220,10 +216,8 @@
     contact_pick = jnp.where(pair_v[...] == slot, 1.0, 0.0)
     slot_picks = (face_pick.astype(BF16), contact_pick.astype(BF16))
 
-    def prepare_slots(kind):
-        source = (ftiles, ctiles)[kind]
-
-        def turn_four(i, carry):
+    def prepare_slots(i, carry):
+        for kind, source in enumerate((ftiles, ctiles)):
             parts = []
             for n in range(4):
                 parts += [source[4 * i + n]] * 2
@@ -235,16 +229,18 @@
                     ef[pl.ds(kind * 16 * PAD + s2 * 64 + 4 * i + n, 16, stride=PAD), :] = jnp.where(
                         low_half((16, 128)), y[at : at + 16], y[at + 16 : at + 32]
                     )
-            return carry
-
-        def pack_slots(i, carry):
-            at = pl.ds(pl.multiple_of(i * 128, 128), 128)
-            e[at, :] = ef[pl.ds(pl.multiple_of(i * PAD, 8), 128), :].astype(BF16)
-            return carry
-
-        fetches[kind].wait()
-        lax.fori_loop(0, 16, turn_four, 0, unroll=4)
-        lax.fori_loop(16 * kind, 16 * kind + 16, pack_slots, 0, unroll=4)
+        return carry
+
+    for fetch in fetches[:2]:
+        fetch.wait()
+    lax.fori_loop(0, 16, prepare_slots, 0, unroll=2)
+
+    def pack_slots(i, carry):
+        at = pl.ds(pl.multiple_of(i * 128, 128), 128)
+        e[at, :] = ef[pl.ds(pl.multiple_of(i * PAD, 8), 128), :].astype(BF16)
+        return carry
+
+    lax.fori_loop(0, 32, pack_slots, 0, unroll=4)
 
     def tile_at(ref, index):
         return ref[pl.ds(pl.multiple_of(index * 128, 128), 128), :]
@@ -303,8 +299,6 @@
 
     def transpose_slots(app):
         copies = []
-        if app == 0:
-            prepare_slots(0)
         for kind, rows in enumerate((lambda i: frows_s[i], lambda i: crows_s[0, i])):
 
             def body(tp, carry):
@@ -327,9 +321,6 @@
             if app == 0 and kind == 0:
                 pl.semaphore_wait(barrier, len(everyone))
             copies += exchange(app, kind)
-            if app == 0 and kind == 0:
-                order_contacts()
-                prepare_slots(1)
         return copies
 
     def transpose_inner(field):
@@ -373,14 +364,10 @@
         low = low_half((128, 128))
         z = zs[...] + dot(ohs[...], halves([rbuf[app, np] for np in range(4)]))
         if send_app is not None:
-            terms = jnp.concatenate(split(z), axis=0)
-            copies = []
-            for kind in range(2):
-                at = slice(64 * kind, 64 * kind + 64)
-                x = dot(ohst[at], terms)
-                for np in range(4):
-                    sbuf[send_app, np, at] = x[:, 128 * np : 128 * np + 128]
-                copies += exchange(send_app, kind)
+            x = dot(ohst[...], jnp.concatenate(split(z), axis=0))
+            for np in range(4):
+                sbuf[send_app, np] = x[:, 128 * np : 128 * np + 128]
+            copies = exchange(send_app, 0) + exchange(send_app, 1)
         for np in range(4):
             x = z[:, 128 * np : 128 * np + 128]
             if result is None:
@@ -459,7 +446,6 @@
         return jnp.broadcast_to(x[None], (rows // 8, 8, 128)).reshape(rows, 128)
 
     copies = transpose_slots(0)
-    prepare_picks()
     prepare_inner()
     transpose_inner(f0)
     copies = transpose_end(0, copies, z0, 1)

time: 56.4 us -> 55.1 us (0.977)
  Pallas kernels: 55.6 us -> 54.3 us
    pallas_call x1, Pallas kernels: 53.6 us -> 52.3 us  [shards(): pl.pallas_call(functools.partial(kernel, devices), out_shape=[out] * 3, i...]
where the time goes in v5:
time: 55.1 us; the launch traced here: 55 us
  Pallas kernels  54.3 us (99%)
  between operations  0.64 us (1%)
    pallas_call x1, Pallas kernels, shards(): pl.pallas_call(functools.partial(kernel, devices), out_shape=[out] * 3, i...  52.3 us
    pallas_call x1, Pallas kernels, shards(): pl.pallas_call(hand_over, out_shape=[out] * 3, in_specs=[vmem] * 3, out_s...  2 us

profile of v5, /device:TPU:1, one launch (start us, length us, event | category | flops | bytes accessed | tf_op | source)
XLA Modules:
  0.0 55.0 jit_solution(1113242413926834054)
XLA Ops:
  0.6 52.3 %shard_map.130 = (f32[512,128]{1,0:T(8,128)}, f32[512,128]{1,0:T(8,128)}, f32[512,128]{1,0:T(8,128)}) custom-call(s32[4,128]{1,0:T(4,128)} %cols_v.1, s32[64]{0:T(128)} %frows_s.1, s32[1,2]{1,0:T(1,128)} %counts_s.1, f32[512,128]{1,0:T(8,128)} %bitcast.8, s32[4,128]{1,0:T(4,128)} %cols_v.1, s32[1,64]{1,0:T(1,128)} %bitcast.10, s32[1,64]{1,0:T(1,128)} %bitcast.11, ...), custom_call_target="tpu_custom_call" | custom-call | tf_op jit(solution)/shard_map/pallas_call | solution.py:533
  53.0 2.0 %shard_map.131 = (f32[512,128]{1,0:T(8,128)}, f32[512,128]{1,0:T(8,128)}, f32[512,128]{1,0:T(8,128)}) custom-call(f32[512,128]{1,0:T(8,128)} %get-tuple-element.9.refs_0_, f32[512,128]{1,0:T(8,128)} %get-tuple-element.10.refs_1_, f32[512,128]{1,0:T(8,128)} %get-tuple-element.11.refs_2_), custom_call_target="tpu_custom_call" | custom-call | tf_op jit(solution)/shard_map/pallas_call | solution.py:594

commit v6 on v5

--- a/solution.py
+++ b/solution.py
@@ -233,14 +233,14 @@
 
     for fetch in fetches[:2]:
         fetch.wait()
-    lax.fori_loop(0, 16, prepare_slots, 0, unroll=2)
+    lax.fori_loop(0, 16, prepare_slots, 0, unroll=4)
 
     def pack_slots(i, carry):
         at = pl.ds(pl.multiple_of(i * 128, 128), 128)
         e[at, :] = ef[pl.ds(pl.multiple_of(i * PAD, 8), 128), :].astype(BF16)
         return carry
 
-    lax.fori_loop(0, 32, pack_slots, 0, unroll=4)
+    lax.fori_loop(0, 32, pack_slots, 0, unroll=8)
 
     def tile_at(ref, index):
         return ref[pl.ds(pl.multiple_of(index * 128, 128), 128), :]

time: 55.1 us -> 54.3 us (0.985)
  Pallas kernels: 54.3 us -> 53.6 us
    pallas_call x1, Pallas kernels: 52.3 us -> 51.6 us  [shards(): pl.pallas_call(functools.partial(kernel, devices), out_shape=[out] * 3, i...]
where the time goes in v6:
time: 54.3 us; the launch traced here: 54.2 us
  Pallas kernels  53.6 us (99%)
  between operations  0.64 us (1%)
    pallas_call x1, Pallas kernels, shards(): pl.pallas_call(functools.partial(kernel, devices), out_shape=[out] * 3, i...  51.6 us
    pallas_call x1, Pallas kernels, shards(): pl.pallas_call(hand_over, out_shape=[out] * 3, in_specs=[vmem] * 3, out_s...  2 us

profile of v6, /device:TPU:1, one launch (start us, length us, event | category | flops | bytes accessed | tf_op | source)
XLA Modules:
  0.0 54.2 jit_solution(5390182677125643396)
XLA Ops:
  0.6 51.6 %shard_map.130 = (f32[512,128]{1,0:T(8,128)}, f32[512,128]{1,0:T(8,128)}, f32[512,128]{1,0:T(8,128)}) custom-call(s32[4,128]{1,0:T(4,128)} %cols_v.1, s32[64]{0:T(128)} %frows_s.1, s32[1,2]{1,0:T(1,128)} %counts_s.1, f32[512,128]{1,0:T(8,128)} %bitcast.8, s32[4,128]{1,0:T(4,128)} %cols_v.1, s32[1,64]{1,0:T(1,128)} %bitcast.10, s32[1,64]{1,0:T(1,128)} %bitcast.11, ...), custom_call_target="tpu_custom_call" | custom-call | tf_op jit(solution)/shard_map/pallas_call | solution.py:533
  52.2 2.0 %shard_map.131 = (f32[512,128]{1,0:T(8,128)}, f32[512,128]{1,0:T(8,128)}, f32[512,128]{1,0:T(8,128)}) custom-call(f32[512,128]{1,0:T(8,128)} %get-tuple-element.9.refs_0_, f32[512,128]{1,0:T(8,128)} %get-tuple-element.10.refs_1_, f32[512,128]{1,0:T(8,128)} %get-tuple-element.11.refs_2_), custom_call_target="tpu_custom_call" | custom-call | tf_op jit(solution)/shard_map/pallas_call | solution.py:594
